TPU v7x, 32 devices: a whole 2x2x4 slice. The times are simulated.
32 devices in a mesh: ctx: 4 (over y, x), tp: 8 (over z, core).
Axes of the slice: x: 2, y: 2, z: 4, core: 2. Of those that a mesh axis runs over, the one named last changes fastest.
Arguments:
- layer_in: bfloat16 [4096, 2048], P('ctx', 'tp'), may hold values from -6 to 6
- gain_attn: float32 [2048], replicated, may hold values from 0.5 to 1.5
- gain_ffn: float32 [2048], replicated, may hold values from 0.5 to 1.5
- w_query: bfloat16 [2048, 1024], P(None, 'tp'), may hold values from -0.1875 to 0.1875
- w_key: bfloat16 [2048, 1024], P(None, 'tp'), may hold values from -0.1875 to 0.1875
- w_value: bfloat16 [2048, 1024], P(None, 'tp'), may hold values from -0.125 to 0.125
- w_out: bfloat16 [1024, 2048], P('tp'), may hold values from -1.5 to 1.5
- w_gate: bfloat16 [2048, 4096], P(None, 'tp'), may hold values from -0.125 to 0.125
- w_up: bfloat16 [2048, 4096], P(None, 'tp'), may hold values from -0.125 to 0.125
- w_down: bfloat16 [4096, 2048], P('tp'), may hold values from -0.09375 to 0.09375
- doc_ids: int32 [4096], P('ctx'), may hold values from 0 to 3, as said below
- positions: int32 [4096], P('ctx'), may hold values from 0 to 3071, as said below
- cotangent: bfloat16 [4096, 2048], P('ctx', 'tp'), may hold values from -6 to 6
Outputs:
- out: bfloat16 [4096, 2048], P('ctx', 'tp')
- grad_input: float32 [4096, 2048], P('ctx', 'tp')
- grad_gain_attn: float32 [2048], P('tp')
- grad_gain_ffn: float32 [2048], P('tp')
- grad_query: float32 [2048, 1024], P(None, 'tp')
- grad_key: float32 [2048, 1024], P(None, 'tp')
- grad_value: float32 [2048, 1024], P(None, 'tp')
- grad_out: float32 [1024, 2048], P('tp')
- grad_gate: float32 [2048, 4096], P(None, 'tp')
- grad_up: float32 [2048, 4096], P(None, 'tp')
- grad_down: float32 [4096, 2048], P('tp')
Inputs may be any that keep to these rules, and one draw needn't show every extreme that they name: `doc_ids`: never falls along the sequence; four documents, starting at 0. `positions`: 0 at a document's first token and rising by one within the document.
All inputs are finite; a program needn't handle non-finite values.
Results may differ from a plain program's by a relative error of at most 0.013.
The roundings to bfloat16 on the way count: a program that leaves them out, or rounds other values in their place, can miss the bound.
Values may be sent and summed in bfloat16 or wider, within the bound.
No kernel may reach another device: no remote copies, remote signals or barrier semaphores. Data moves between devices by JAX's collectives and lax.ppermute only.
A program may use at most 192 MiB of HBM per device.

v0:
```python
import math

import jax
import jax.numpy as jnp
from jax import lax
from jax.sharding import PartitionSpec as P

HDIM = 128


EPS = 1e-05
THETA = 10000.0


def rope_tables(places, width):
    half_width = width // 2
    freq = THETA ** (-(jnp.arange(half_width, dtype=jnp.float32) * 2.0 / width))
    angle = places.astype(jnp.float32)[:, None] * freq[None, :]
    return (jnp.cos(angle)[:, None, :], jnp.sin(angle)[:, None, :])


def rotate(values, cosine, sine_table):
    half_width = values.shape[-1] // 2
    first = values[..., :half_width]
    second = values[..., half_width:]
    return jnp.concatenate(
        [first * cosine - second * sine_table, first * sine_table + second * cosine], axis=-1
    )


def rotate_back(values, cosine, sine_table):
    half_width = values.shape[-1] // 2
    first = values[..., :half_width]
    second = values[..., half_width:]
    return jnp.concatenate(
        [first * cosine + second * sine_table, second * cosine - first * sine_table], axis=-1
    )


def per_device(
    layer_in,
    gain_attn,
    gain_ffn,
    w_query,
    w_key,
    w_value,
    w_out,
    w_gate,
    w_up,
    w_down,
    doc_ids,
    positions,
    cotangent,
):
    tok_rows = layer_in.shape[0]
    share = layer_in.shape[1]
    heads = w_query.shape[1] // HDIM
    head_width = heads * HDIM
    ctx_rank = lax.axis_index("ctx")
    offset = lax.axis_index("tp") * share
    seq_len = tok_rows * lax.axis_size("ctx")
    score_scale = 1.0 / math.sqrt(HDIM)
    score_bias = -math.log(seq_len)
    key_span = math.gcd(seq_len, 512)
    full_in, full_cot = (
        lax.all_gather(layer_in, "tp", axis=1, tiled=True),
        lax.all_gather(cotangent, "tp", axis=1, tiled=True),
    )
    x_full = full_in.astype(jnp.float32)
    cot_full = full_cot.astype(jnp.float32)
    inv_one = lax.rsqrt(jnp.mean(x_full * x_full, axis=-1, keepdims=True) + EPS)
    x_hat = x_full * inv_one
    normed = (x_hat * gain_attn).astype(jnp.bfloat16)
    q_pre = jnp.dot(normed, w_query, preferred_element_type=jnp.float32)
    k_pre = jnp.dot(normed, w_key, preferred_element_type=jnp.float32)
    values = jnp.dot(normed, w_value, preferred_element_type=jnp.float32).astype(jnp.bfloat16)
    cosine, sine_table = rope_tables(positions, HDIM)
    q_rot = rotate(q_pre.reshape(tok_rows, heads, HDIM), cosine, sine_table).astype(jnp.bfloat16)
    k_rot = rotate(k_pre.reshape(tok_rows, heads, HDIM), cosine, sine_table).astype(jnp.bfloat16)
    kv_local = jnp.concatenate([k_rot.reshape(tok_rows, head_width), values], axis=1)
    kv_whole, doc_whole = (
        lax.all_gather(kv_local, "ctx", axis=0, tiled=True),
        lax.all_gather(doc_ids, "ctx", axis=0, tiled=True),
    )
    query_index = ctx_rank * tok_rows + jnp.arange(tok_rows, dtype=jnp.int32)
    visits = ((ctx_rank + 1) * tok_rows + key_span - 1) // key_span

    def scores_block(block_index):
        start = block_index * key_span
        kv_block = lax.dynamic_slice_in_dim(kv_whole, start, key_span, 0)
        doc_block = lax.dynamic_slice_in_dim(doc_whole, start, key_span, 0)
        key_rows = kv_block[:, :head_width].reshape(key_span, heads, HDIM)
        value_rows = kv_block[:, head_width:].reshape(key_span, heads, HDIM)
        scores = (
            jnp.einsum("qhd,khd->hqk", q_rot, key_rows, preferred_element_type=jnp.float32)
            * score_scale
            + score_bias
        )
        key_index = start + jnp.arange(key_span, dtype=jnp.int32)
        visible = (doc_ids[:, None] == doc_block[None, :]) & (
            key_index[None, :] <= query_index[:, None]
        )
        return (key_rows, value_rows, visible[None], jax.nn.sigmoid(scores))

    def forward_step(block_index, total):
        key_rows, value_rows, visible, sig_scores = scores_block(block_index)
        weights = jnp.where(visible, sig_scores, 0.0).astype(jnp.bfloat16)
        return total + jnp.einsum(
            "hqk,khd->qhd", weights, value_rows, preferred_element_type=jnp.float32
        )

    mixed_sum = lax.fori_loop(
        0, visits, forward_step, jnp.zeros((tok_rows, heads, HDIM), jnp.float32)
    )
    mixed = mixed_sum.reshape(tok_rows, head_width).astype(jnp.bfloat16)
    attn_term = jnp.dot(mixed, w_out, preferred_element_type=jnp.float32)
    middle_full = x_full + lax.psum(attn_term, "tp")
    inv_two = lax.rsqrt(jnp.mean(middle_full * middle_full, axis=-1, keepdims=True) + EPS)
    mid_hat = middle_full * inv_two
    normed_two = (mid_hat * gain_ffn).astype(jnp.bfloat16)
    gate_pre = jnp.dot(normed_two, w_gate, preferred_element_type=jnp.float32)
    up_proj = jnp.dot(normed_two, w_up, preferred_element_type=jnp.float32)
    gate_sig = jax.nn.sigmoid(gate_pre)
    hidden = (gate_pre * gate_sig * up_proj).astype(jnp.bfloat16)
    ffn_term = jnp.dot(hidden, w_down, preferred_element_type=jnp.float32)
    out_full = middle_full + lax.psum(ffn_term.astype(jnp.bfloat16), "tp").astype(jnp.float32)
    result = lax.dynamic_slice_in_dim(out_full, offset, share, 1)
    grad_down = jnp.einsum("tf,td->fd", hidden, full_cot, preferred_element_type=jnp.float32)
    g_hidden = jnp.einsum("td,fd->tf", full_cot, w_down, preferred_element_type=jnp.float32)
    g_gate = (g_hidden * up_proj * gate_sig * (1.0 + gate_pre * (1.0 - gate_sig))).astype(
        jnp.bfloat16
    )
    g_up = (g_hidden * gate_pre * gate_sig).astype(jnp.bfloat16)
    grad_gate = jnp.einsum("td,tf->df", normed_two, g_gate, preferred_element_type=jnp.float32)
    grad_up = jnp.einsum("td,tf->df", normed_two, g_up, preferred_element_type=jnp.float32)
    dn2_term = jnp.einsum(
        "tf,df->td", g_gate, w_gate, preferred_element_type=jnp.float32
    ) + jnp.einsum("tf,df->td", g_up, w_up, preferred_element_type=jnp.float32)
    g_normed_two = lax.psum(dn2_term, "tp")
    scaled_two = g_normed_two * gain_ffn
    g_middle = cot_full + inv_two * (
        scaled_two - mid_hat * jnp.mean(scaled_two * mid_hat, axis=-1, keepdims=True)
    )
    grad_gain_two = lax.dynamic_slice_in_dim(
        jnp.sum(g_normed_two * mid_hat, axis=0), offset, share, 0
    )
    g_mid_b = g_middle.astype(jnp.bfloat16)
    grad_out = jnp.einsum("tk,td->kd", mixed, g_mid_b, preferred_element_type=jnp.float32)
    g_mixed = (
        jnp.einsum("td,kd->tk", g_mid_b, w_out, preferred_element_type=jnp.float32)
        .astype(jnp.bfloat16)
        .reshape(tok_rows, heads, HDIM)
    )

    def backward_step(block_index, state_pair):
        g_query_sum, g_kv = state_pair
        key_rows, value_rows, visible, sig_scores = scores_block(block_index)
        weights = jnp.where(visible, sig_scores, 0.0).astype(jnp.bfloat16)
        g_values = jnp.einsum("hqk,qhd->khd", weights, g_mixed, preferred_element_type=jnp.float32)
        g_weights = jnp.einsum(
            "qhd,khd->hqk", g_mixed, value_rows, preferred_element_type=jnp.float32
        )
        g_scores = jnp.where(visible, g_weights * sig_scores * (1.0 - sig_scores), 0.0).astype(
            jnp.bfloat16
        )
        g_query_sum = g_query_sum + jnp.einsum(
            "hqk,khd->qhd", g_scores, key_rows, preferred_element_type=jnp.float32
        )
        g_keys = jnp.einsum("hqk,qhd->khd", g_scores, q_rot, preferred_element_type=jnp.float32)
        g_block = jnp.concatenate(
            [
                g_keys.reshape(key_span, head_width) * score_scale,
                g_values.reshape(key_span, head_width),
            ],
            axis=1,
        )
        return (
            g_query_sum,
            lax.dynamic_update_slice_in_dim(g_kv, g_block, block_index * key_span, 0),
        )

    g_query_sum, g_kv_term = lax.fori_loop(
        0,
        visits,
        backward_step,
        (
            jnp.zeros((tok_rows, heads, HDIM), jnp.float32),
            jnp.zeros((seq_len, 2 * head_width), jnp.float32),
        ),
    )
    g_kv_own = lax.psum_scatter(g_kv_term, "ctx", scatter_dimension=0, tiled=True)
    g_query = (
        rotate_back(g_query_sum * score_scale, cosine, sine_table)
        .reshape(tok_rows, head_width)
        .astype(jnp.bfloat16)
    )
    g_key = (
        rotate_back(g_kv_own[:, :head_width].reshape(tok_rows, heads, HDIM), cosine, sine_table)
        .reshape(tok_rows, head_width)
        .astype(jnp.bfloat16)
    )
    g_value = g_kv_own[:, head_width:].astype(jnp.bfloat16)
    grad_query = jnp.einsum("td,tk->dk", normed, g_query, preferred_element_type=jnp.float32)
    grad_key = jnp.einsum("td,tk->dk", normed, g_key, preferred_element_type=jnp.float32)
    grad_value = jnp.einsum("td,tk->dk", normed, g_value, preferred_element_type=jnp.float32)
    dn1_term = (
        jnp.einsum("tk,dk->td", g_query, w_query, preferred_element_type=jnp.float32)
        + jnp.einsum("tk,dk->td", g_key, w_key, preferred_element_type=jnp.float32)
        + jnp.einsum("tk,dk->td", g_value, w_value, preferred_element_type=jnp.float32)
    )
    g_normed_one = lax.psum(dn1_term, "tp")
    scaled_one = g_normed_one * gain_attn
    g_input_full = g_middle + inv_one * (
        scaled_one - x_hat * jnp.mean(scaled_one * x_hat, axis=-1, keepdims=True)
    )
    g_input = lax.dynamic_slice_in_dim(g_input_full, offset, share, 1)
    grad_gain_one = lax.dynamic_slice_in_dim(
        jnp.sum(g_normed_one * x_hat, axis=0), offset, share, 0
    )
    summed = lax.psum(
        (
            grad_query,
            grad_key,
            grad_value,
            grad_out,
            grad_gate,
            grad_up,
            grad_down,
            grad_gain_one,
            grad_gain_two,
        ),
        "ctx",
    )
    return (
        result.astype(jnp.bfloat16),
        g_input,
        summed[7],
        summed[8],
        summed[0],
        summed[1],
        summed[2],
        summed[3],
        summed[4],
        summed[5],
        summed[6],
    )


def solution(mesh):
    in_specs = (
        P("ctx", "tp"),
        P(),
        P(),
        P(None, "tp"),
        P(None, "tp"),
        P(None, "tp"),
        P("tp", None),
        P(None, "tp"),
        P(None, "tp"),
        P("tp", None),
        P("ctx"),
        P("ctx"),
        P("ctx", "tp"),
    )
    out_specs = (
        P("ctx", "tp"),
        P("ctx", "tp"),
        P("tp"),
        P("tp"),
        P(None, "tp"),
        P(None, "tp"),
        P(None, "tp"),
        P("tp", None),
        P(None, "tp"),
        P(None, "tp"),
        P("tp", None),
    )
    return jax.shard_map(
        per_device, mesh=mesh, in_specs=in_specs, out_specs=out_specs, check_vma=False
    )
```

profile of v0, /device:TPU:0, one launch (start us, length us, event | category | flops | bytes accessed | tf_op | source)
XLA Modules:
  0.0 1314.0 jit_solution(12290888014087614681)
XLA Ops:
  8.7 51.5 %all-gather.4.cloned.1.call-done = bf16[1024,2048]{1,0:T(8,128)(2,1)} async-done(((bf16[1024,256]{1,0:T(8,128)(2,1)}), bf16[1024,2048]{1,0:T(8,128)(2,1)}) %all-gather.4.cloned.1.call-update) | async-done | bytes 4194320 | tf_op jit(solution)/shard_map/all_gather | solution.py:66
  74.7 8.2 all_gather.14
  83.1 25.3 %all-gather.6.cloned.1.call-done = bf16[4096,256]{0,1:T(8,128)(2,1)} async-done(((bf16[1024,256]{0,1:T(8,128)(2,1)}), bf16[4096,256]{0,1:T(8,128)(2,1)}) %all-gather.6.cloned.1.call-update) | async-done | bytes 2097168 | tf_op jit(solution)/shard_map/all_gather | solution.py:82
  116.9 4.6 fusion.92
  122.3 188.1 %all-reduce.8.cloned.1.call-done = f32[1024,2048]{1,0:T(8,128)} async-done(((f32[1024,2048]{1,0:T(8,128)}), f32[1024,2048]{1,0:T(8,128)}) %all-reduce.8.cloned.1.call-update) | async-done | bytes 8388624 | tf_op jit(solution)/shard_map/psum | solution.py:117
  310.4 5.7 multiply_reduce_fusion.4
  327.5 32.4 %all-gather.8.cloned.1.call-done = bf16[1024,2048]{1,0:T(8,128)(2,1)} async-done(((bf16[1024,256]{1,0:T(8,128)(2,1)}), bf16[1024,2048]{1,0:T(8,128)(2,1)}) %all-gather.8.cloned.1.call-update) | async-done | bytes 4194320 | tf_op jit(solution)/shard_map/all_gather | solution.py:67
  359.8 7.7 multiply_convert_fusion.2
  370.0 5.6 convolution_add_fusion
  376.1 173.5 %all-reduce.12.cloned.1.call-done = f32[1024,2048]{1,0:T(8,128)} async-done(((f32[1024,2048]{1,0:T(8,128)}), f32[1024,2048]{1,0:T(8,128)}) %all-reduce.12.cloned.1.call-update) | async-done | bytes 8388624 | tf_op jit(solution)/shard_map/psum | solution.py:139
  549.6 7.1 multiply_reduce_fusion
  559.0 4.6 multiply_add_fusion
  569.5 17.8 %while.25 = (s32[]{:T(128)}, f32[1024,1,128]{0,2,1:T(8,128)S(1)}, f32[4096,256]{0,1:T(8,128)}, s32[]{:T(128)}, bf16[4096,256]{1,0:T(8,128)(2,1)}, /*index=5*/s32...) while((s32[]{:T(128)}, f32[1024,1,128]{0,2,1:T(8,128)S(1)}, ...), condition=%wide.region_9.10_spmd.clone, body=%wide.region_8.9_spmd.clone.sunk | while | flops 680330752 | bytes 22972712 | solution.py:182
  587.4 5.6 convolution_convert_fusion
  593.9 99.9 %reduce-scatter.2.cloned.1.call-done = f32[1024,256]{0,1:T(8,128)} async-done(((f32[4096,256]{0,1:T(8,128)}), f32[1024,256]{0,1:T(8,128)}) %reduce-scatter.2.cloned.1.call-update) | async-done | bytes 1048592 | tf_op jit(solution)/shard_map/reduce_scatter | solution.py:191
  700.8 4.6 add_add_fusion
  705.7 7.1 fusion.110
  712.8 4.5 fusion.111
  717.3 4.5 fusion.112
  731.3 62.1 %all-reduce.10.cloned.1.call-done = bf16[1024,2048]{1,0:T(8,128)(2,1)} async-done(((bf16[1024,2048]{1,0:T(8,128)(2,1)}), bf16[1024,2048]{1,0:T(8,128)(2,1)}) %all-reduce.10.cloned.1.call-update) | async-done | bytes 4194320 | tf_op jit(solution)/shard_map/psum | solution.py:126
  795.7 175.8 %all-reduce.14.cloned.1.call-done = f32[1024,2048]{1,0:T(8,128)} async-done(((f32[1024,2048]{1,0:T(8,128)}), f32[1024,2048]{1,0:T(8,128)}) %all-reduce.14.cloned.1.call-update) | async-done | bytes 8388624 | tf_op jit(solution)/shard_map/psum | solution.py:211
  971.5 7.7 multiply_reduce_fusion.1
  979.4 10.6 all-reduce
  993.2 298.0 %all-reduce.16.cloned.1.call-done = (f32[2048,128]{1,0:T(8,128)}, f32[2048,128]{1,0:T(8,128)}, f32[2048,128]{1,0:T(8,128)}, f32[128,2048]{1,0:T(8,128)}, f32[204...) async-done(((f32[2048,128]{1,0:T(8,128)}, f32[2048,128]{1,0:T(8,128)}, f32[2048,128]{1,0:T(8,128)}, f32[128,2048]{1,0:T(8,128)}, f32[2048,512]{1,0:T(8,128)}, ...) | async-done | bytes 16777232 | tf_op jit(solution)/shard_map/psum | solution.py:220
  (178 shorter events, 109.3 us)
Async XLA Ops:
  7.2 352.6 %copy-start = (bf16[512,2048]{1,0:T(8,128)(2,1)S(1)}, bf16[512,2048]{1,0:T(8,128)(2,1)}, u32[]{:S(2)}) copy-start(bf16[512,2048]{1,0:T(8,128)(2,1)} %param.26) | copy-start | bytes 6291460
  7.2 56.2 %copy-start.33 = (f32[2048]{0:T(1024)S(1)}, f32[2048]{0:T(1024)}, u32[]{:S(2)}) copy-start(f32[2048]{0:T(1024)} %param.18) | copy-start | bytes 24580
  7.2 53.0 %all-gather.4.cloned.1.call-start = ((), (), s32[]{:S(2)}) async-start(), calls=%async_computation.1 | async-start | bytes 4718592 | tf_op jit(solution)/shard_map/all_gather | solution.py:66
  7.9 100.4 %all-gather.6.cloned.1.call-start = ((), (), s32[]{:S(2)}) async-start(), calls=%async_computation.2 | async-start | bytes 2621440 | tf_op jit(solution)/shard_map/all_gather | solution.py:82
  74.7 235.8 %all-reduce.8.cloned.1.call-start = ((), (), s32[]{:S(2)}) async-start(), calls=%async_computation.3 | async-start | bytes 16777216 | tf_op jit(solution)/shard_map/psum | solution.py:117
  121.5 238.3 %all-gather.8.cloned.1.call-start = ((), (), s32[]{:S(2)}) async-start(), calls=%async_computation.5 | async-start | bytes 4718592 | tf_op jit(solution)/shard_map/all_gather | solution.py:67
  122.1 194.1 %copy-start.30 = (f32[2048]{0:T(1024)S(1)}, f32[2048]{0:T(1024)}, u32[]{:S(2)}) copy-start(f32[2048]{0:T(1024)} %param.19) | copy-start | bytes 24580
  122.1 427.5 %all-reduce.12.cloned.1.call-start = ((), (), s32[]{:S(2)}) async-start(), calls=%async_computation.6 | async-start | bytes 16777216 | tf_op jit(solution)/shard_map/psum | solution.py:139
  359.8 7.7 copy-start.37
  375.6 318.2 %reduce-scatter.2.cloned.1.call-start = ((), (), s32[]{:S(2)}) async-start(), calls=%async_computation.7 | async-start | bytes 5242880 | tf_op jit(solution)/shard_map/reduce_scatter | solution.py:191
  549.6 8.2 copy-start.6
  549.6 9.4 copy-start.7
  587.4 206.0 %all-reduce.10.cloned.1.call-start = ((), (), s32[]{:S(2)}) async-start(), calls=%async_computation.4 | async-start | bytes 8388608 | tf_op jit(solution)/shard_map/psum | solution.py:126
  593.0 378.5 %all-reduce.14.cloned.1.call-start = ((), (), s32[]{:S(2)}) async-start(), calls=%async_computation.8 | async-start | bytes 16777216 | tf_op jit(solution)/shard_map/psum | solution.py:211
  705.4 585.7 %all-reduce.16.cloned.1.call-start = ((), (), s32[]{:S(2)}) async-start(), calls=%async_computation.9 | async-start | bytes 33554432 | tf_op jit(solution)/shard_map/psum | solution.py:220
  705.7 7.1 copy-start.10
  705.7 7.1 copy-start.15
  705.7 16.1 %slice-start = ((s8[8388608]{0:T(1024)(128)(4,1)}), s8[4194304]{0:T(1024)(128)(4,1)S(1)}, s32[]{:S(2)}) async-start(s8[8388608]{0:T(1024)(128)(4,1)} %bitcast.138), calls=%async_computation.10 | async-start | bytes 8388608
  712.8 9.0 slice-start.1
  731.3 240.2 %copy-start.32 = (f32[1024]{0:T(1024)S(1)}, f32[1024]{0:T(1024)}, u32[]{:S(2)}) copy-start(f32[1024]{0:T(1024)} %copy-done.31) | copy-start | bytes 12292
  731.3 240.2 %copy-start.34 = (f32[2048]{0:T(1024)S(1)}, f32[2048]{0:T(1024)}, u32[]{:S(2)}) copy-start(f32[2048]{0:T(1024)} %param.18) | copy-start | bytes 24580
  1291.2 4.8 copy-start.28
  1291.2 5.8 copy-start.27
  1291.2 6.7 copy-start.13
  (29 other events, 95.4 us)
Sparse Core Ops, SparseCore 0:
  9.6 50.4 all-gather.3
  74.8 33.5 all-gather.5
  121.6 188.7 all-reduce.7
  311.9 47.9 all-gather.7
  375.7 173.7 all-reduce.11
  587.5 106.2 reduce-scatter.1
  696.9 96.4 all-reduce.9
  795.9 175.6 all-reduce.13
  978.2 312.9 all-reduce.15
where the time goes:
time: 1320 us; the launch traced here: 1310 us
  waiting for transfers between devices  1110 us (84%)
  matrix products  93.2 us (7%)
  other arithmetic  46.5 us (4%)
  local copies, waits for them, and re-layouts  32.1 us (2%)
  blocking collectives  18.8 us (1%)
  between operations  14.5 us (1%)
    psum x1, waiting for transfers between devices, per_device(): lax.psum((grad_query, grad_key, grad_value, grad_out, grad_gate, grad_up,...  298 us
    psum x1, waiting for transfers between devices, per_device(): middle_full = x_full + lax.psum(attn_term, 'tp')  188 us
    psum x1, waiting for transfers between devices, per_device(): g_normed_one = lax.psum(dn1_term, 'tp')  176 us
    psum x1, waiting for transfers between devices, per_device(): g_normed_two = lax.psum(dn2_term, 'tp')  173 us
    reduce_scatter x1, waiting for transfers between devices, per_device(): lax.psum_scatter(g_kv_term, 'ctx', scatter_dimension=0, tiled=True)  99.9 us
    psum x1, waiting for transfers between devices, per_device(): lax.psum(ffn_term.astype(jnp.bfloat16), 'tp').astype(jnp.float32)  62.1 us
    all_gather x1, waiting for transfers between devices, per_device(): lax.all_gather(layer_in, 'tp', axis=1, tiled=True)  51.5 us
    all_gather x1, waiting for transfers between devices, per_device(): lax.all_gather(cotangent, 'tp', axis=1, tiled=True)  32.4 us
  transfers between devices with their start and end apart: 9, of which 9 were waited for; matrix products, arithmetic and copies ran while one was open for 5% of the time, Pallas kernels for 0%

commit v1 on v0

v1 whole, which is shorter than its diff:
```python
import math

import jax
import jax.numpy as jnp
from jax import lax
from jax.sharding import PartitionSpec as P

HDIM = 128
EPS = 1e-05
THETA = 10000.0
BF = jnp.bfloat16
F32 = jnp.float32


def rope_tables(places, width):
    half_width = width // 2
    freq = THETA ** (-(jnp.arange(half_width, dtype=F32) * 2.0 / width))
    angle = places.astype(F32)[:, None] * freq[None, :]
    return jnp.cos(angle), jnp.sin(angle)


def rotate(values, cosine, sine):
    half = values.shape[-1] // 2
    first, second = values[..., :half], values[..., half:]
    return jnp.concatenate([first * cosine - second * sine, first * sine + second * cosine], axis=-1)


def rotate_back(values, cosine, sine):
    half = values.shape[-1] // 2
    first, second = values[..., :half], values[..., half:]
    return jnp.concatenate([first * cosine + second * sine, second * cosine - first * sine], axis=-1)


def dot(a, b, dims, out=F32):
    return lax.dot_general(a, b, (dims, ((), ())), preferred_element_type=F32).astype(out)


NN = ((1,), (0,))
NT = ((1,), (1,))
TN = ((0,), (0,))


def folded(n):
    return [0] + list(range(1, n, 2)) + list(range(n - 2 + n % 2, 0, -2))


class Tp:
    def __init__(self, n_tp):
        self.n = n_tp
        self.pairs = n_tp // 2
        self.ring = folded(self.pairs)
        place = [self.ring.index(z) for z in range(self.pairs)]
        self.core_perm = [(i, i ^ 1) for i in range(n_tp)]
        self.ring_perm = []
        for i in range(n_tp):
            z, c = divmod(i, 2)
            self.ring_perm.append((i, self.ring[(place[z] + 1) % self.pairs] * 2 + c))
        order, where = [], []
        for i in range(n_tp):
            z, c = divmod(i, 2)
            row = []
            for j in range(self.pairs):
                src = self.ring[(place[z] - j) % self.pairs]
                row += [src * 2 + c, src * 2 + 1 - c]
            order.append(row)
            where.append([row.index(b) for b in range(n_tp)])
        me = lax.axis_index("tp")
        self.order = [jnp.asarray([order[i][k] for i in range(n_tp)], jnp.int32)[me] for k in range(n_tp)]
        self.where = [jnp.asarray([where[i][k] for i in range(n_tp)], jnp.int32)[me] for k in range(n_tp)]

    def core(self, a):
        return lax.ppermute(a, "tp", self.core_perm)

    def step(self, a):
        return lax.ppermute(a, "tp", self.ring_perm)

    def gather(self, block):
        got, cur = [], block
        for j in range(self.pairs):
            if j:
                cur = self.step(cur)
            got += [cur, self.core(cur)]
        return got

    def scatter(self, partial):
        share = partial.shape[1] // self.n
        acc = None
        for j in list(range(1, self.pairs)) + [0]:
            own = partial[:, 2 * j * share : (2 * j + 1) * share].astype(F32)
            other = self.core(partial[:, (2 * j + 1) * share : (2 * j + 2) * share])
            term = own + other.astype(F32)
            if acc is not None:
                term = term + self.step(acc.astype(BF)).astype(F32)
            acc = term
        return acc

    def total(self, small):
        out = small + self.core(small)
        cur, acc = out, out
        for _ in range(1, self.pairs):
            cur = self.step(cur)
            acc = acc + cur
        return acc

    def to_ring(self, a, axis):
        size = a.shape[axis] // self.n
        return jnp.concatenate(
            [lax.dynamic_slice_in_dim(a, k * size, size, axis) for k in self.order], axis=axis
        )

    def from_ring(self, a, axis):
        size = a.shape[axis] // self.n
        return jnp.concatenate(
            [lax.dynamic_slice_in_dim(a, k * size, size, axis) for k in self.where], axis=axis
        )


def per_device(
    layer_in,
    gain_attn,
    gain_ffn,
    w_query,
    w_key,
    w_value,
    w_out,
    w_gate,
    w_up,
    w_down,
    doc_ids,
    positions,
    cotangent,
):
    tok, share = layer_in.shape
    n_ctx, n_tp = lax.axis_size("ctx"), lax.axis_size("tp")
    width = share * n_tp
    heads = w_query.shape[1] // HDIM
    head_width = heads * HDIM
    hid = w_gate.shape[1]
    tp = Tp(n_tp)
    rank = lax.axis_index("ctx")
    own = lax.axis_index("tp") * share
    seq_len = tok * n_ctx
    score_scale = 1.0 / math.sqrt(HDIM)
    score_bias = -math.log(seq_len)
    span = math.gcd(tok, 512)

    gain_a_own = lax.dynamic_slice_in_dim(gain_attn, own, share, 0)
    gain_f_own = lax.dynamic_slice_in_dim(gain_ffn, own, share, 0)
    gain_a = tp.to_ring(gain_attn, 0)
    gain_f = tp.to_ring(gain_ffn, 0)
    wqkv = tp.to_ring(jnp.concatenate([w_query, w_key, w_value], axis=1), 0)
    wo = tp.to_ring(w_out, 1)
    wgu = tp.to_ring(jnp.concatenate([w_gate, w_up], axis=1), 0)
    wd = tp.to_ring(w_down, 1)

    x_full = jnp.concatenate(tp.gather(layer_in), axis=1)
    x_wide = x_full.astype(F32)
    r1 = lax.rsqrt(jnp.mean(x_wide * x_wide, axis=-1, keepdims=True) + EPS)
    normed = (x_wide * r1 * gain_a).astype(BF)
    qkv = dot(normed, wqkv, NN)
    q_pre, k_pre, v_pre = jnp.split(qkv, 3, axis=1)
    cosine, sine = rope_tables(positions, HDIM)
    cosine, sine = cosine[:, None, :], sine[:, None, :]
    q_rot = rotate(q_pre.reshape(tok, heads, HDIM), cosine, sine).astype(BF)
    k_rot = rotate(k_pre.reshape(tok, heads, HDIM), cosine, sine).astype(BF)
    values = v_pre.astype(BF)
    kv_own = jnp.concatenate([k_rot.reshape(tok, head_width), values], axis=1)

    def shift(a, s):
        return lax.ppermute(a, "ctx", [(r, r + s) for r in range(n_ctx) if 0 <= r + s < n_ctx])

    kv_all = jnp.concatenate([shift(kv_own, s) for s in range(n_ctx - 1, 0, -1)] + [kv_own], axis=0)
    base = (rank - (n_ctx - 1)) * tok
    q_index = rank * tok + jnp.arange(tok, dtype=jnp.int32)
    q_start = q_index - positions
    first = jnp.maximum((q_start[0] - base) // span, 0)
    last = seq_len // span

    def scores_block(b):
        kv = lax.dynamic_slice_in_dim(kv_all, b * span, span, 0)
        keys = kv[:, :head_width].reshape(span, heads, HDIM)
        vals = kv[:, head_width:].reshape(span, heads, HDIM)
        s = jnp.einsum("qhd,khd->hqk", q_rot, keys, preferred_element_type=F32)
        s = s * score_scale + score_bias
        k_index = base + b * span + jnp.arange(span, dtype=jnp.int32)
        visible = (k_index[None, :] >= q_start[:, None]) & (k_index[None, :] <= q_index[:, None])
        return keys, vals, visible[None], jax.nn.sigmoid(s)

    def forward_step(b, total):
        keys, vals, visible, sig = scores_block(b)
        weights = jnp.where(visible, sig, 0.0).astype(BF)
        return total + jnp.einsum("hqk,khd->qhd", weights, vals, preferred_element_type=F32)

    mixed = lax.fori_loop(first, last, forward_step, jnp.zeros((tok, heads, HDIM), F32))
    mixed = mixed.reshape(tok, head_width).astype(BF)

    h = layer_in.astype(F32) + tp.scatter(dot(mixed, wo, NN, BF))

    cot_full = jnp.concatenate(tp.gather(cotangent), axis=1)
    hg_full = jnp.concatenate(tp.gather((h * gain_f_own).astype(BF)), axis=1)
    h_wide = hg_full.astype(F32) * (1.0 / gain_f)
    r2 = lax.rsqrt(jnp.mean(h_wide * h_wide, axis=-1, keepdims=True) + EPS)
    pre = dot(hg_full, wgu, NN) * r2
    gate, up = pre[:, :hid], pre[:, hid:]
    sig = jax.nn.sigmoid(gate)
    silu = gate * sig
    hidden = (silu * up).astype(BF)
    g_hidden = dot(cot_full, wd, NT)
    g_gate = g_hidden * up * sig * (1.0 + gate * (1.0 - sig))
    g_up = g_hidden * silu
    m2 = tp.total(jnp.sum(g_gate * gate + g_up * up, axis=-1)) / width
    ggu = (jnp.concatenate([g_gate, g_up], axis=1) * r2).astype(BF)
    dn2 = tp.scatter(dot(ggu, wgu, NT, BF))
    grad_down = dot(hidden, cot_full, TN, BF)
    grad_gu = dot(hg_full, ggu, TN, BF)
    g_h = cotangent.astype(F32) + gain_f_own * dn2 - (r2 * r2 * m2[:, None]) * h
    grad_gain_two = jnp.sum(dn2 * h, axis=0)
    out = h + tp.scatter(dot(hidden, wd, NN, BF))

    g_hb = jnp.concatenate(tp.gather(g_h.astype(BF)), axis=1)
    grad_out = dot(mixed, g_hb, TN, BF)
    g_mixed = dot(g_hb, wo, NT, BF).reshape(tok, heads, HDIM)

    def backward_step(b, state):
        g_query_sum, g_kv = state
        keys, vals, visible, sig = scores_block(b)
        weights = jnp.where(visible, sig, 0.0).astype(BF)
        g_values = jnp.einsum("hqk,qhd->khd", weights, g_mixed, preferred_element_type=F32)
        g_weights = jnp.einsum("qhd,khd->hqk", g_mixed, vals, preferred_element_type=F32)
        g_scores = jnp.where(visible, g_weights * sig * (1.0 - sig), 0.0).astype(BF)
        g_query_sum = g_query_sum + jnp.einsum("hqk,khd->qhd", g_scores, keys, preferred_element_type=F32)
        g_keys = jnp.einsum("hqk,qhd->khd", g_scores, q_rot, preferred_element_type=F32)
        g_block = jnp.concatenate(
            [g_keys.reshape(span, head_width) * score_scale, g_values.reshape(span, head_width)], axis=1
        )
        return g_query_sum, lax.dynamic_update_slice_in_dim(g_kv, g_block, b * span, 0)

    g_query, g_kv_all = lax.fori_loop(
        first,
        last,
        backward_step,
        (jnp.zeros((tok, heads, HDIM), F32), jnp.zeros((seq_len, 2 * head_width), F32)),
    )
    g_kv = g_kv_all[-tok:]
    for s in range(n_ctx - 1, 0, -1):
        at = (n_ctx - 1 - s) * tok
        g_kv = g_kv + shift(g_kv_all[at : at + tok].astype(BF), -s).astype(F32)
    g_query = rotate_back(g_query * score_scale, cosine, sine).reshape(tok, head_width)
    g_key = rotate_back(g_kv[:, :head_width].reshape(tok, heads, HDIM), cosine, sine).reshape(tok, head_width)
    g_qkv = jnp.concatenate([g_query, g_key, g_kv[:, head_width:]], axis=1)
    m1 = tp.total(jnp.sum(g_qkv * qkv, axis=-1)) / width
    g_qkv = g_qkv.astype(BF)
    grad_qkv = dot(normed, g_qkv, TN, BF)
    dn1 = tp.scatter(dot(g_qkv, wqkv, NT, BF))
    x_own = layer_in.astype(F32)
    x_hat = x_own * r1
    g_input = g_h + r1 * (dn1 * gain_a_own - x_hat * m1[:, None])
    grad_gain_one = jnp.sum(dn1 * x_hat, axis=0)

    grad_down, grad_gu = lax.psum((grad_down, grad_gu), "ctx")
    grad_out, grad_qkv = lax.psum((grad_out, grad_qkv), "ctx")
    gains = lax.psum(jnp.concatenate([grad_gain_one, grad_gain_two]), "ctx")
    grad_qkv = tp.from_ring(grad_qkv, 0).astype(F32)
    grad_gu = tp.from_ring(grad_gu, 0).astype(F32)
    return (
        out.astype(BF),
        g_input,
        gains[:share],
        gains[share:],
        grad_qkv[:, :head_width],
        grad_qkv[:, head_width : 2 * head_width],
        grad_qkv[:, 2 * head_width :],
        tp.from_ring(grad_out, 1).astype(F32),
        grad_gu[:, :hid],
        grad_gu[:, hid:],
        tp.from_ring(grad_down, 1).astype(F32),
    )


def solution(mesh):
    row, col = P("tp", None), P(None, "tp")
    both = P("ctx", "tp")
    in_specs = (both, P(), P(), col, col, col, row, col, col, row, P("ctx"), P("ctx"), both)
    out_specs = (both, both, P("tp"), P("tp"), col, col, col, row, col, col, row)
    return jax.shard_map(
        per_device, mesh=mesh, in_specs=in_specs, out_specs=out_specs, check_vma=False
    )
```

time: 1320 us -> 684 us (0.52)
  waiting for transfers between devices: 1110 us -> 384 us
  local copies, waits for them, and re-layouts: 32.1 us -> 80.9 us
  starting transfers between devices: 1.12 us -> 48.4 us
  matrix products: 93.2 us -> 75.5 us
    psum x5 -> x1, waiting for transfers between devices: 897 us -> 60.2 us  [per_device(): grad_out, grad_qkv = lax.psum((grad_out, grad_qkv), 'ctx')]
    ppermute x0 -> x70, waiting for transfers between devices: none -> 323 us  [the longest x30 237 us: step(): return lax.ppermute(a, 'tp', self.ring_perm)]
    all_gather x3 -> x0, waiting for transfers between devices: 109 us -> none  [the longest x1 51.5 us: per_device(): lax.all_gather(layer_in, 'tp', axis=1, tiled=True)]
    reduce_scatter x1 -> x0, waiting for transfers between devices: 99.9 us -> none  [per_device(): lax.psum_scatter(g_kv_term, 'ctx', scatter_dimension=0, tiled=True)]
    ppermute x0 -> x70, starting transfers between devices: none -> 48.4 us  [the longest x30 29.1 us: step(): return lax.ppermute(a, 'tp', self.ring_perm)]
    unnamed x89 -> x181, local copies, waits for them, and re-layouts: 28 us -> 48.8 us
    dot_general x33 -> x24, matrix products: 93.2 us -> 75.5 us  [the longest x12 60 us: dot(): lax.dot_general(a, b, (dims, ((), ())), preferred_element_type=F32)]
    dynamic_slice x6 -> x16, local copies, waits for them, and re-layouts: 0.45 us -> 14 us  [the longest x7 8.71 us: __init__(): jnp.asarray([order[i][k] for i in range(n_tp)], jnp.int32)[me]]
  transfers between devices with their start and end apart: 9 -> 71, of which waited for: 9 -> 33; matrix products, arithmetic and copies ran while one was open for 5% -> 17% of each run, Pallas kernels for 0% -> 0%
where the time goes in v1:
time: 684 us; the launch traced here: 674 us
  waiting for transfers between devices  384 us (56%)
  local copies, waits for them, and re-layouts  80.9 us (12%)
  matrix products  75.5 us (11%)
  starting transfers between devices  48.4 us (7%)
  other arithmetic  40.1 us (6%)
  between operations  26.6 us (4%)
  blocking collectives  18 us (3%)
    ppermute x30, waiting for transfers between devices, step(): return lax.ppermute(a, 'tp', self.ring_perm)  237 us
    ppermute x6, waiting for transfers between devices, shift(): lax.ppermute(a, 'ctx', [(r, r + s) for r in range(n_ctx) if 0 <= r + s <...  79.4 us
    psum x1, waiting for transfers between devices, per_device(): grad_out, grad_qkv = lax.psum((grad_out, grad_qkv), 'ctx')  60.2 us
    dot_general x12, matrix products, dot(): lax.dot_general(a, b, (dims, ((), ())), preferred_element_type=F32)  60 us
    unnamed x181, local copies, waits for them, and re-layouts  48.8 us
    ppermute x30, starting transfers between devices, step(): return lax.ppermute(a, 'tp', self.ring_perm)  29.1 us
    psum x1, blocking collectives, per_device(): gains = lax.psum(jnp.concatenate([grad_gain_one, grad_gain_two]), 'ctx')  18 us
    ppermute x6, starting transfers between devices, shift(): lax.ppermute(a, 'ctx', [(r, r + s) for r in range(n_ctx) if 0 <= r + s <...  13.8 us
  transfers between devices with their start and end apart: 71, of which 33 were waited for; matrix products, arithmetic and copies ran while one was open for 17% of the time, Pallas kernels for 0%

profile of v1, /device:TPU:0, one launch (start us, length us, event | category | flops | bytes accessed | tf_op | source)
XLA Modules:
  0.0 673.7 jit_solution(9029204128517995408)
XLA Ops:
  44.5 11.2 %collective-permute-done.3 = bf16[1024,256]{1,0:T(8,128)(2,1)} collective-permute-done((bf16[1024,256]{1,0:T(8,128)(2,1)S(1)}, bf16[1024,256]{1,0:T(8,128)(2,1)}, u32[]{:S(2)}, u32[]{:S(2)}) %collective-permute-start.3) | collective-permute-done | bytes 524320 | tf_op jit(solution)/shard_map/ppermute | solution.py:75
  101.6 11.8 %collective-permute-done.8 = bf16[1024,256]{0,1:T(8,128)(2,1)} collective-permute-done((bf16[1024,256]{0,1:T(8,128)(2,1)S(1)}, bf16[1024,256]{0,1:T(8,128)(2,1)}, u32[]{:S(2)}, u32[]{:S(2)}) %collective-permute-start.8) | collective-permute-done | bytes 524320 | tf_op jit(solution)/shard_map/ppermute | solution.py:170
  113.4 9.1 %maximum_maximum_fusion = bf16[4096,256]{0,1:T(8,128)(2,1)S(1)} fusion(bf16[1024,128]{0,1:T(8,128)(2,1)S(1)} %split.19, bf16[1024,64]{0,1:T(8,128)(2,1)S(1)} %get-tuple-element.261, bf16[1024,64]{0,1:T(8,128)(2,1)S(1)} %get-tuple-element.262, bf16[1024,256]{0,1:T(8,128)(2,1)} %copy-done.24, bf16[1024,256]{0,1:T(8,128)(2,1)} %collective-permute-done.8, ...), kind=kLoop, calls=%fused_computation.68 | loop fusion | flops 12582912 | bytes 4194304 | tf_op jit(solution)/shard_map/concatenate | solution.py:172
  136.4 13.6 %collective-permute-done.14 = bf16[1024,256]{1,0:T(8,128)(2,1)S(1)} collective-permute-done((bf16[1024,256]{1,0:T(8,128)(2,1)S(1)}, bf16[1024,256]{1,0:T(8,128)(2,1)S(1)}, u32[]{:S(2)}, u32[]{:S(2)}) %collective-permute-start.14) | collective-permute-done | bytes 524320 | tf_op jit(solution)/shard_map/ppermute | solution.py:75
  150.7 14.0 %collective-permute-done.15 = bf16[1024,256]{1,0:T(8,128)(2,1)S(1)} collective-permute-done((bf16[1024,256]{1,0:T(8,128)(2,1)S(1)}, bf16[1024,256]{1,0:T(8,128)(2,1)S(1)}, u32[]{:S(2)}, u32[]{:S(2)}) %collective-permute-start.15) | collective-permute-done | bytes 524320 | tf_op jit(solution)/shard_map/ppermute | solution.py:75
  168.3 12.5 %collective-permute-done.16 = bf16[1024,256]{1,0:T(8,128)(2,1)S(1)} collective-permute-done((bf16[1024,256]{1,0:T(8,128)(2,1)S(1)}, bf16[1024,256]{1,0:T(8,128)(2,1)S(1)}, u32[]{:S(2)}, u32[]{:S(2)}) %collective-permute-start.16) | collective-permute-done | bytes 524320 | tf_op jit(solution)/shard_map/ppermute | solution.py:75
  181.3 10.7 %collective-permute-done.34 = bf16[1024,256]{1,0:T(8,128)(2,1)S(1)} collective-permute-done((bf16[1024,256]{1,0:T(8,128)(2,1)}, bf16[1024,256]{1,0:T(8,128)(2,1)S(1)}, u32[]{:S(2)}, u32[]{:S(2)}) %collective-permute-start.34) | collective-permute-done | bytes 524320 | tf_op jit(solution)/shard_map/ppermute | solution.py:75
  192.2 11.1 %collective-permute-done.18 = bf16[1024,256]{1,0:T(8,128)(2,1)S(1)} collective-permute-done((bf16[1024,256]{1,0:T(8,128)(2,1)S(1)}, bf16[1024,256]{1,0:T(8,128)(2,1)S(1)}, u32[]{:S(2)}, u32[]{:S(2)}) %collective-permute-start.18) | collective-permute-done | bytes 524320 | tf_op jit(solution)/shard_map/ppermute | solution.py:75
  204.9 9.6 %collective-permute-done.36 = bf16[1024,256]{1,0:T(8,128)(2,1)S(1)} collective-permute-done((bf16[1024,256]{1,0:T(8,128)(2,1)S(1)}, bf16[1024,256]{1,0:T(8,128)(2,1)S(1)}, u32[]{:S(2)}, u32[]{:S(2)}) %collective-permute-start.36) | collective-permute-done | bytes 524320 | tf_op jit(solution)/shard_map/ppermute | solution.py:75
  224.4 11.6 %collective-permute-done.22 = bf16[1024,256]{1,0:T(8,128)(2,1)S(1)} collective-permute-done((bf16[1024,256]{1,0:T(8,128)(2,1)S(1)}, bf16[1024,256]{1,0:T(8,128)(2,1)S(1)}, u32[]{:S(2)}, u32[]{:S(2)}) %collective-permute-start.22) | collective-permute-done | bytes 524320 | tf_op jit(solution)/shard_map/ppermute | solution.py:75
  250.4 17.4 %convolution_convert_fusion.4 = bf16[1024,2048]{1,0:T(8,128)(2,1)S(1)} fusion(bf16[2048,1024]{1,0:T(8,128)(2,1)} %copy-done.25, f32[1024,512]{0,1:T(8,128)} %get-tuple-element.210, f32[1024,512]{0,1:T(8,128)S(1)} %get-tuple-element.209, f32[1024]{0:T(1024)S(1)} %add_rsqrt_fusion), kind=kOutput, calls=%fused_computation.63 | convolution fusion | flops 4300210176 | bytes 12587008 | tf_op jit(solution)/shard_map/dot_general | solution.py:35
  270.7 14.4 %collective-permute-done.42 = bf16[1024,256]{1,0:T(8,128)(2,1)S(1)} collective-permute-done((bf16[1024,256]{1,0:T(8,128)(2,1)S(1)}, bf16[1024,256]{1,0:T(8,128)(2,1)S(1)}, u32[]{:S(2)}, u32[]{:S(2)}) %collective-permute-start.42) | collective-permute-done | bytes 524320 | tf_op jit(solution)/shard_map/ppermute | solution.py:75
  285.4 13.9 %collective-permute-done.43 = bf16[1024,256]{1,0:T(8,128)(2,1)S(1)} collective-permute-done((bf16[1024,256]{1,0:T(8,128)(2,1)S(1)}, bf16[1024,256]{1,0:T(8,128)(2,1)S(1)}, u32[]{:S(2)}, u32[]{:S(2)}) %collective-permute-start.43) | collective-permute-done | bytes 524320 | tf_op jit(solution)/shard_map/ppermute | solution.py:75
  303.8 9.0 %collective-permute-done.46 = f32[1024]{0:T(1024)S(1)} collective-permute-done((f32[1024]{0:T(1024)S(1)}, f32[1024]{0:T(1024)S(1)}, u32[]{:S(2)}, u32[]{:S(2)}) %collective-permute-start.46) | collective-permute-done | bytes 4128 | tf_op jit(solution)/shard_map/ppermute | solution.py:75
  324.5 12.5 %collective-permute-done.50 = bf16[1024,256]{1,0:T(8,128)(2,1)S(1)} collective-permute-done((bf16[1024,256]{1,0:T(8,128)(2,1)S(1)}, bf16[1024,256]{1,0:T(8,128)(2,1)S(1)}, u32[]{:S(2)}, u32[]{:S(2)}) %collective-permute-start.50) | collective-permute-done | bytes 524320 | tf_op jit(solution)/shard_map/ppermute | solution.py:75
  367.7 13.0 %while.25 = (s32[]{:T(128)}, f32[1024,1,128]{0,2,1:T(8,128)S(1)}, f32[4096,256]{0,1:T(8,128)}, bf16[4096,256]{1,0:T(8,128)(2,1)}, s32[]{:T(128)}, /*index=5*/s32...) while((s32[]{:T(128)}, f32[1024,1,128]{0,2,1:T(8,128)S(1)}, ...), condition=%wide.region_6.7_spmd.clone, body=%wide.region_5.6_spmd.clone.sunk | while | flops 680330752 | bytes 14575875 | solution.py:238
  389.2 64.6 %collective-permute-done.56 = bf16[1024,256]{0,1:T(8,128)(2,1)S(1)} collective-permute-done((bf16[1024,256]{0,1:T(8,128)(2,1)S(1)}, bf16[1024,256]{0,1:T(8,128)(2,1)S(1)}, u32[]{:S(2)}, u32[]{:S(2)}) %collective-permute-start.56) | collective-permute-done | bytes 524320 | tf_op jit(solution)/shard_map/ppermute | solution.py:170
  476.0 12.2 %collective-permute-done.28 = bf16[1024,256]{1,0:T(8,128)(2,1)S(1)} collective-permute-done((bf16[1024,256]{1,0:T(8,128)(2,1)S(1)}, bf16[1024,256]{1,0:T(8,128)(2,1)S(1)}, u32[]{:S(2)}, u32[]{:S(2)}) %collective-permute-start.28) | collective-permute-done | bytes 524320 | tf_op jit(solution)/shard_map/ppermute | solution.py:75
  489.5 9.9 %collective-permute-done.63 = bf16[1024,256]{1,0:T(8,128)(2,1)S(1)} collective-permute-done((bf16[1024,256]{1,0:T(8,128)(2,1)S(1)}, bf16[1024,256]{1,0:T(8,128)(2,1)S(1)}, u32[]{:S(2)}, u32[]{:S(2)}) %collective-permute-start.63) | collective-permute-done | bytes 524320 | tf_op jit(solution)/shard_map/ppermute | solution.py:75
  501.4 9.2 %collective-permute-done.29 = bf16[1024,256]{1,0:T(8,128)(2,1)S(1)} collective-permute-done((bf16[1024,256]{1,0:T(8,128)(2,1)S(1)}, bf16[1024,256]{1,0:T(8,128)(2,1)S(1)}, u32[]{:S(2)}, u32[]{:S(2)}) %collective-permute-start.29) | collective-permute-done | bytes 524320 | tf_op jit(solution)/shard_map/ppermute | solution.py:75
  516.3 16.0 %collective-permute-done.67 = f32[1024]{0:T(1024)S(1)} collective-permute-done((f32[1024]{0:T(1024)S(1)}, f32[1024]{0:T(1024)S(1)}, u32[]{:S(2)}, u32[]{:S(2)}) %collective-permute-start.67) | collective-permute-done | bytes 4128 | tf_op jit(solution)/shard_map/ppermute | solution.py:75
  550.6 11.7 %collective-permute-done.65 = bf16[1024,256]{1,0:T(8,128)(2,1)S(1)} collective-permute-done((bf16[1024,256]{1,0:T(8,128)(2,1)S(1)}, bf16[1024,256]{1,0:T(8,128)(2,1)S(1)}, u32[]{:S(2)}, u32[]{:S(2)}) %collective-permute-start.65) | collective-permute-done | bytes 524320 | tf_op jit(solution)/shard_map/ppermute | solution.py:75
  564.9 18.0 %psum.35 = f32[512]{0:T(512)S(1)} all-reduce(f32[512]{0:T(512)S(1)} %pad_maximum_fusion.3), channel_id=1, replica_groups=mesh['ctx'=4,'tp'=8] {'ctx'}, use_global_device_ids=true, to_apply=%region_10.11 | all-reduce | flops 512 | bytes 4096 | tf_op jit(solution)/shard_map/psum | solution.py:262
  583.5 60.2 %all-reduce.3.cloned.1.call-done = (bf16[2048,384]{1,0:T(8,128)(2,1)}, bf16[128,2048]{1,0:T(8,128)(2,1)}, bf16[2048,1024]{1,0:T(8,128)(2,1)}, bf16[512,2048]{1,0:T(8,128)(2,1)}) async-done(((bf16[2048,384]{1,0:T(8,128)(2,1)}, bf16[128,2048]{1,0:T(8,128)(2,1)}, bf16[2048,1024]{1,0:T(8,128)(2,1)}, bf16[512,2048]{1,0:T(8,128)(2,1)}), (bf16[2048,384]{1,0:T(8,128)(2,1)}, bf16[128,2048]{1,0:T(8,128)(2,1)}, ...) | async-done | bytes 8388624 | tf_op jit(solution)/shard_map/psum | solution.py:261
  (431 shorter events, 267.4 us)
Async XLA Ops:
  7.2 636.5 %all-reduce.3.cloned.1.call-start = ((), (), s32[]{:S(2)}) async-start(), calls=%async_computation | async-start | bytes 16777216 | tf_op jit(solution)/shard_map/psum | solution.py:261
  7.3 52.8 %collective-permute-start = (bf16[1024,256]{1,0:T(8,128)(2,1)}, bf16[1024,256]{1,0:T(8,128)(2,1)}, u32[]{:S(2)}, u32[]{:S(2)}) collective-permute-start(bf16[1024,256]{1,0:T(8,128)(2,1)} %param.33), channel_id=1, source_target_pairs={{0,1},{1,0},{2,3},{3,2},{4,5},{5,4},{6,7},{7,6},{8,9},{9,8},{10,11... | collective-permute-start | bytes 1572872 | tf_op jit(solution)/shard_map/ppermute | solution.py:72
  7.8 32.7 %collective-permute-start.1 = (bf16[1024,256]{1,0:T(8,128)(2,1)}, bf16[1024,256]{1,0:T(8,128)(2,1)S(1)}, u32[]{:S(2)}, u32[]{:S(2)}) collective-permute-start(bf16[1024,256]{1,0:T(8,128)(2,1)} %param.33), channel_id=1, source_target_pairs={{0,2},{1,3},{2,6},{3,7},{4,0},{5,1},{6,4},{7,5},{8,10},{9,11},{10,... | collective-permute-start | bytes 1572872 | tf_op jit(solution)/shard_map/ppermute | solution.py:75
  10.4 193.0 %collective-permute-start.31 = (bf16[1024,256]{1,0:T(8,128)(2,1)}, bf16[1024,256]{1,0:T(8,128)(2,1)}, u32[]{:S(2)}, u32[]{:S(2)}) collective-permute-start(bf16[1024,256]{1,0:T(8,128)(2,1)} %param.44), channel_id=1, source_target_pairs={{0,1},{1,0},{2,3},{3,2},{4,5},{5,4},{6,7},{7,6},{8,9},{9,8},{10,11... | collective-permute-start | bytes 1572872 | tf_op jit(solution)/shard_map/ppermute | solution.py:72
  60.1 105.1 %collective-permute-start.32 = (bf16[1024,256]{1,0:T(8,128)(2,1)}, bf16[1024,256]{1,0:T(8,128)(2,1)}, u32[]{:S(2)}, u32[]{:S(2)}) collective-permute-start(bf16[1024,256]{1,0:T(8,128)(2,1)} %param.44), channel_id=1, source_target_pairs={{0,2},{1,3},{2,6},{3,7},{4,0},{5,1},{6,4},{7,5},{8,10},{9,11},{10,... | collective-permute-start | bytes 1572872 | tf_op jit(solution)/shard_map/ppermute | solution.py:75
  89.4 24.0 %collective-permute-start.8 = (bf16[1024,256]{0,1:T(8,128)(2,1)S(1)}, bf16[1024,256]{0,1:T(8,128)(2,1)}, u32[]{:S(2)}, u32[]{:S(2)}) collective-permute-start(bf16[1024,256]{0,1:T(8,128)(2,1)S(1)} %pad_maximum_fusion.1), channel_id=1, source_target_pairs={{0,16},{8,24},{1,17},{9,25},{2,18},{10,26},{3,19},{11,27},{4,20},{... | collective-permute-start | bytes 1572872 | tf_op jit(solution)/shard_map/ppermute | solution.py:170
  165.2 26.8 %collective-permute-start.34 = (bf16[1024,256]{1,0:T(8,128)(2,1)}, bf16[1024,256]{1,0:T(8,128)(2,1)S(1)}, u32[]{:S(2)}, u32[]{:S(2)}) collective-permute-start(bf16[1024,256]{1,0:T(8,128)(2,1)} %collective-permute-done.32), channel_id=1, source_target_pairs={{0,2},{1,3},{2,6},{3,7},{4,0},{5,1},{6,4},{7,5},{8,10},{9,11},{10,... | collective-permute-start | bytes 1572872 | tf_op jit(solution)/shard_map/ppermute | solution.py:75
  181.1 22.1 %collective-permute-start.18 = (bf16[1024,256]{1,0:T(8,128)(2,1)S(1)}, bf16[1024,256]{1,0:T(8,128)(2,1)S(1)}, u32[]{:S(2)}, u32[]{:S(2)}) collective-permute-start(bf16[1024,256]{1,0:T(8,128)(2,1)S(1)} %get-tuple-element.212), channel_id=1, source_target_pairs={{0,2},{1,3},{2,6},{3,7},{4,0},{5,1},{6,4},{7,5},{8,10},{9,11},{10,... | collective-permute-start | bytes 1572872 | tf_op jit(solution)/shard_map/ppermute | solution.py:75
  192.0 22.5 %collective-permute-start.36 = (bf16[1024,256]{1,0:T(8,128)(2,1)S(1)}, bf16[1024,256]{1,0:T(8,128)(2,1)S(1)}, u32[]{:S(2)}, u32[]{:S(2)}) collective-permute-start(bf16[1024,256]{1,0:T(8,128)(2,1)S(1)} %collective-permute-done.34), channel_id=1, source_target_pairs={{0,2},{1,3},{2,6},{3,7},{4,0},{5,1},{6,4},{7,5},{8,10},{9,11},{10,... | collective-permute-start | bytes 1572872 | tf_op jit(solution)/shard_map/ppermute | solution.py:75
  192.0 24.1 %collective-permute-start.33 = (bf16[1024,256]{1,0:T(8,128)(2,1)}, bf16[1024,256]{1,0:T(8,128)(2,1)S(1)}, u32[]{:S(2)}, u32[]{:S(2)}) collective-permute-start(bf16[1024,256]{1,0:T(8,128)(2,1)} %collective-permute-done.32), channel_id=1, source_target_pairs={{0,1},{1,0},{2,3},{3,2},{4,5},{5,4},{6,7},{7,6},{8,9},{9,8},{10,11... | collective-permute-start | bytes 1572872 | tf_op jit(solution)/shard_map/ppermute | solution.py:72
  203.2 20.2 %collective-permute-start.20 = (bf16[1024,256]{1,0:T(8,128)(2,1)S(1)}, bf16[1024,256]{1,0:T(8,128)(2,1)S(1)}, u32[]{:S(2)}, u32[]{:S(2)}) collective-permute-start(bf16[1024,256]{1,0:T(8,128)(2,1)S(1)} %collective-permute-done.18), channel_id=1, source_target_pairs={{0,2},{1,3},{2,6},{3,7},{4,0},{5,1},{6,4},{7,5},{8,10},{9,11},{10,... | collective-permute-start | bytes 1572872 | tf_op jit(solution)/shard_map/ppermute | solution.py:75
  203.3 20.3 %collective-permute-start.35 = (bf16[1024,256]{1,0:T(8,128)(2,1)S(1)}, bf16[1024,256]{1,0:T(8,128)(2,1)S(1)}, u32[]{:S(2)}, u32[]{:S(2)}) collective-permute-start(bf16[1024,256]{1,0:T(8,128)(2,1)S(1)} %collective-permute-done.34), channel_id=1, source_target_pairs={{0,1},{1,0},{2,3},{3,2},{4,5},{5,4},{6,7},{7,6},{8,9},{9,8},{10,11... | collective-permute-start | bytes 1572872 | tf_op jit(solution)/shard_map/ppermute | solution.py:72
  285.3 36.6 %collective-permute-start.38 = (bf16[1024,256]{1,0:T(8,128)(2,1)S(1)}, bf16[1024,256]{1,0:T(8,128)(2,1)S(1)}, u32[]{:S(2)}, u32[]{:S(2)}) collective-permute-start(bf16[1024,256]{1,0:T(8,128)(2,1)S(1)} %get-tuple-element.222), channel_id=1, source_target_pairs={{0,1},{1,0},{2,3},{3,2},{4,5},{5,4},{6,7},{7,6},{8,9},{9,8},{10,11... | collective-permute-start | bytes 1572872 | tf_op jit(solution)/shard_map/ppermute | solution.py:72
  299.6 22.3 %collective-permute-start.44 = (bf16[1024,256]{1,0:T(8,128)(2,1)S(1)}, bf16[1024,256]{1,0:T(8,128)(2,1)S(1)}, u32[]{:S(2)}, u32[]{:S(2)}) collective-permute-start(bf16[1024,256]{1,0:T(8,128)(2,1)S(1)} %add_convert_fusion.3), channel_id=1, source_target_pairs={{0,2},{1,3},{2,6},{3,7},{4,0},{5,1},{6,4},{7,5},{8,10},{9,11},{10,... | collective-permute-start | bytes 1572872 | tf_op jit(solution)/shard_map/ppermute | solution.py:75
  383.5 70.3 %collective-permute-start.56 = (bf16[1024,256]{0,1:T(8,128)(2,1)S(1)}, bf16[1024,256]{0,1:T(8,128)(2,1)S(1)}, u32[]{:S(2)}, u32[]{:S(2)}) collective-permute-start(bf16[1024,256]{0,1:T(8,128)(2,1)S(1)} %get-tuple-element.235), channel_id=1, source_target_pairs={{24,0},{25,1},{26,2},{27,3},{28,4},{29,5},{30,6},{31,7}} | collective-permute-start | bytes 1572872 | tf_op jit(solution)/shard_map/ppermute | solution.py:170
  384.8 69.0 %collective-permute-start.58 = (bf16[1024,256]{0,1:T(8,128)(2,1)S(1)}, bf16[1024,256]{0,1:T(8,128)(2,1)S(1)}, u32[]{:S(2)}, u32[]{:S(2)}) collective-permute-start(bf16[1024,256]{0,1:T(8,128)(2,1)S(1)} %get-tuple-element.236), channel_id=1, source_target_pairs={{8,0},{16,8},{24,16},{9,1},{17,9},{25,17},{10,2},{18,10},{26,18},{... | collective-permute-start | bytes 1572872 | tf_op jit(solution)/shard_map/ppermute | solution.py:170
  386.1 67.7 %collective-permute-start.57 = (bf16[1024,256]{0,1:T(8,128)(2,1)S(1)}, bf16[1024,256]{0,1:T(8,128)(2,1)S(1)}, u32[]{:S(2)}, u32[]{:S(2)}) collective-permute-start(bf16[1024,256]{0,1:T(8,128)(2,1)S(1)} %get-tuple-element.237), channel_id=1, source_target_pairs={{16,0},{24,8},{17,1},{25,9},{18,2},{26,10},{19,3},{27,11},{20,4},{... | collective-permute-start | bytes 1572872 | tf_op jit(solution)/shard_map/ppermute | solution.py:170
  474.6 24.9 %collective-permute-start.63 = (bf16[1024,256]{1,0:T(8,128)(2,1)S(1)}, bf16[1024,256]{1,0:T(8,128)(2,1)S(1)}, u32[]{:S(2)}, u32[]{:S(2)}) collective-permute-start(bf16[1024,256]{1,0:T(8,128)(2,1)S(1)} %add_convert_fusion.2), channel_id=1, source_target_pairs={{0,2},{1,3},{2,6},{3,7},{4,0},{5,1},{6,4},{7,5},{8,10},{9,11},{10,... | collective-permute-start | bytes 1572872 | tf_op jit(solution)/shard_map/ppermute | solution.py:75
  475.8 25.6 %collective-permute-start.25 = (bf16[1024,256]{1,0:T(8,128)(2,1)S(1)}, bf16[1024,256]{1,0:T(8,128)(2,1)S(1)}, u32[]{:S(2)}, u32[]{:S(2)}) collective-permute-start(bf16[1024,256]{1,0:T(8,128)(2,1)S(1)} %get-tuple-element.230), channel_id=1, source_target_pairs={{0,1},{1,0},{2,3},{3,2},{4,5},{5,4},{6,7},{7,6},{8,9},{9,8},{10,11... | collective-permute-start | bytes 1572872 | tf_op jit(solution)/shard_map/ppermute | solution.py:72
  488.5 22.1 %collective-permute-start.29 = (bf16[1024,256]{1,0:T(8,128)(2,1)S(1)}, bf16[1024,256]{1,0:T(8,128)(2,1)S(1)}, u32[]{:S(2)}, u32[]{:S(2)}) collective-permute-start(bf16[1024,256]{1,0:T(8,128)(2,1)S(1)} %add_convert_fusion.8), channel_id=1, source_target_pairs={{0,2},{1,3},{2,6},{3,7},{4,0},{5,1},{6,4},{7,5},{8,10},{9,11},{10,... | collective-permute-start | bytes 1572872 | tf_op jit(solution)/shard_map/ppermute | solution.py:75
  489.5 54.1 %collective-permute-start.60 = (bf16[1024,256]{1,0:T(8,128)(2,1)}, bf16[1024,256]{1,0:T(8,128)(2,1)}, u32[]{:S(2)}, u32[]{:S(2)}) collective-permute-start(bf16[1024,256]{1,0:T(8,128)(2,1)} %get-tuple-element.221), channel_id=1, source_target_pairs={{0,1},{1,0},{2,3},{3,2},{4,5},{5,4},{6,7},{7,6},{8,9},{9,8},{10,11... | collective-permute-start | bytes 1572872 | tf_op jit(solution)/shard_map/ppermute | solution.py:72
  500.5 45.3 %collective-permute-start.64 = (bf16[1024,256]{1,0:T(8,128)(2,1)}, bf16[1024,256]{1,0:T(8,128)(2,1)}, u32[]{:S(2)}, u32[]{:S(2)}) collective-permute-start(bf16[1024,256]{1,0:T(8,128)(2,1)} %add_convert_fusion.1), channel_id=1, source_target_pairs={{0,2},{1,3},{2,6},{3,7},{4,0},{5,1},{6,4},{7,5},{8,10},{9,11},{10,... | collective-permute-start | bytes 1572872 | tf_op jit(solution)/shard_map/ppermute | solution.py:75
  501.4 46.2 %collective-permute-start.24 = (bf16[1024,256]{1,0:T(8,128)(2,1)}, bf16[1024,256]{1,0:T(8,128)(2,1)}, u32[]{:S(2)}, u32[]{:S(2)}) collective-permute-start(bf16[1024,256]{1,0:T(8,128)(2,1)} %get-tuple-element.227), channel_id=1, source_target_pairs={{0,1},{1,0},{2,3},{3,2},{4,5},{5,4},{6,7},{7,6},{8,9},{9,8},{10,11... | collective-permute-start | bytes 1572872 | tf_op jit(solution)/shard_map/ppermute | solution.py:72
  511.7 35.9 %collective-permute-start.30 = (bf16[1024,256]{1,0:T(8,128)(2,1)}, bf16[1024,256]{1,0:T(8,128)(2,1)}, u32[]{:S(2)}, u32[]{:S(2)}) collective-permute-start(bf16[1024,256]{1,0:T(8,128)(2,1)} %add_convert_fusion.7), channel_id=1, source_target_pairs={{0,2},{1,3},{2,6},{3,7},{4,0},{5,1},{6,4},{7,5},{8,10},{9,11},{10,... | collective-permute-start | bytes 1572872 | tf_op jit(solution)/shard_map/ppermute | solution.py:75
  (90 other events, 1697.6 us)
Sparse Core Ops, SparseCore 0:
  460.8 182.8 all-reduce.2

commit v2 on v1

v2 whole, which is shorter than its diff:
```python
import functools
import math

import jax
import jax.numpy as jnp
from jax import lax
from jax.experimental import pallas as pl
from jax.experimental.pallas import tpu as pltpu
from jax.sharding import PartitionSpec as P

HDIM = 128
EPS = 1e-05
THETA = 10000.0
LOG2E = math.log2(math.e)
SCALE = 1.0 / math.sqrt(HDIM)
BF = jnp.bfloat16
F32 = jnp.float32
I32 = jnp.int32
BQ, BK = 512, 512
VMEM_BYTES = 60 * 1024 * 1024
CHUNKS = 1
COST = 1.0

SM = pl.BlockSpec(memory_space=pltpu.SMEM)
VM = pl.BlockSpec(memory_space=pltpu.VMEM)


def shape(dims, dtype):
    return jax.ShapeDtypeStruct(dims, dtype)


def params():
    return pltpu.CompilerParams(vmem_limit_bytes=VMEM_BYTES)


def cost(mults, size):
    return pl.CostEstimate(flops=int(2 * mults * COST), bytes_accessed=int(size * COST), transcendentals=0)


def nn(a, b):
    return lax.dot_general(a, b, (((1,), (0,)), ((), ())), preferred_element_type=F32)


def nt(a, b):
    return lax.dot_general(a, b, (((1,), (1,)), ((), ())), preferred_element_type=F32)


def tn(a, b):
    return lax.dot_general(a, b, (((0,), (0,)), ((), ())), preferred_element_type=F32)


def add(a, b):
    return b if a is None else a + b


def tiles(width, k, n=None):
    return pl.ds(pl.multiple_of(k * width, width), width)


def row_sums(a):
    high = a.astype(BF)
    low = (a - high.astype(F32)).astype(BF)
    ones = jnp.ones((8, a.shape[1]), BF)
    return nt(ones, high) + nt(ones, low)


def qkv_kernel(n, order, *refs):
    xs = refs[:n]
    gain, wq, wk, wv, cos, sin, normed, q, kv, r1_out = refs[n:]
    share = xs[0].shape[1]
    squares = None
    for k in range(n):
        v = xs[k][...].astype(F32)
        squares = add(squares, v * v)
    r1 = lax.rsqrt(jnp.sum(squares, axis=-1, keepdims=True) / (n * share) + EPS)
    sums = [None] * 3
    for k in range(n):
        block = (xs[k][...].astype(F32) * r1 * gain[pl.ds(order[k], 1), :]).astype(BF)
        normed[:, k * share : (k + 1) * share] = block
        rows = tiles(share, order[k])
        for i, w in enumerate((wq, wk, wv)):
            sums[i] = add(sums[i], nn(block, w[rows, :]))
    c, s = cos[...], sin[...]

    def rotated(v):
        return v * c + pltpu.roll(v, HDIM // 2, 1) * s

    q[...] = rotated(sums[0]).astype(BF)
    kv[:, :HDIM] = rotated(sums[1]).astype(BF)
    kv[:, HDIM:] = sums[2].astype(BF)
    r1_out[...] = jnp.broadcast_to(r1, r1_out.shape)


def call_qkv(order, xs, gain, wq, wk, wv, cos, sin):
    n = len(xs)
    tok, share = xs[0].shape
    bt = min(tok, 256)

    def row(w):
        return pl.BlockSpec((bt, w), lambda i, o: (i, 0))

    def full(a):
        return pl.BlockSpec(a.shape, lambda i, o: (0, 0))

    spec = pltpu.PrefetchScalarGridSpec(
        num_scalar_prefetch=1,
        grid=(tok // bt,),
        in_specs=[row(share)] * n + [full(a) for a in (gain, wq, wk, wv)] + [row(HDIM)] * 2,
        out_specs=[row(n * share), row(HDIM), row(2 * HDIM), row(128)],
    )
    return pl.pallas_call(
        functools.partial(qkv_kernel, n),
        grid_spec=spec,
        out_shape=[
            shape((tok, n * share), BF),
            shape((tok, HDIM), BF),
            shape((tok, 2 * HDIM), BF),
            shape((tok, 128), F32),
        ],
        compiler_params=params(),
        cost_estimate=cost(5 * tok * n * share * HDIM * 4, 10 * tok * n * share),
        name="norm_qkv",
    )(order, *xs, gain, wq, wk, wv, cos, sin)


def edges_of(rank, tok, starts):
    t = starts.reshape(tok // BQ, BQ)
    return jnp.concatenate([(rank * tok)[None], jnp.stack([t[:, 0], t[:, -1]], axis=1).reshape(-1)])


def sigmoid_of(raw, bias):
    return 1.0 / (1.0 + jnp.exp2(raw * (-LOG2E * SCALE) - bias * LOG2E))


def own_kernel(bias, tok, edges, start, q, kv, total):
    base = edges[0]
    for qi in range(tok // BQ):
        rows = slice(qi * BQ, (qi + 1) * BQ)
        q_tile = q[rows, :]
        first_key = start[rows, :] - base
        q_index = qi * BQ + lax.broadcasted_iota(I32, (BQ, 1), 0)

        def body(ki, acc):
            at = tiles(BK, ki)
            w = sigmoid_of(nt(q_tile, kv[at, :HDIM]), bias)
            k_index = ki * BK + lax.broadcasted_iota(I32, (BQ, BK), 1)
            w = jnp.where((k_index >= first_key) & (k_index <= q_index), w, 0.0)
            return acc + nn(w.astype(BF), kv[at, HDIM:])

        low = jnp.maximum(edges[1 + 2 * qi] - base, 0) // BK
        high = ((qi + 1) * BQ + BK - 1) // BK
        total[rows, :] = lax.fori_loop(low, high, body, jnp.zeros((BQ, HDIM), F32))


def far_kernel(bias, tok, q0, n_far, n, edges, order, start, q, acc, wo, *refs):
    kvs, mixed, pieces = refs[:n_far], refs[n_far], refs[n_far + 1 :]
    share = wo.shape[1] // n
    n_keys = tok // BK
    for qi in range(q.shape[0] // BQ):
        rows = slice(qi * BQ, (qi + 1) * BQ)
        at_first, at_last = 1 + 2 * (q0 // BQ + qi), 2 + 2 * (q0 // BQ + qi)
        q_tile = q[rows, :]
        total = acc[rows, :]
        for i in range(n_far):
            base = edges[0] - (i + 1) * tok
            kv = kvs[i]
            first_key = start[rows, :] - base

            def body(ki, total, masked):
                at = tiles(BK, ki)
                w = sigmoid_of(nt(q_tile, kv[at, :HDIM]), bias)
                if masked:
                    k_index = ki * BK + lax.broadcasted_iota(I32, (BQ, BK), 1)
                    w = jnp.where(k_index >= first_key, w, 0.0)
                return total + nn(w.astype(BF), kv[at, HDIM:])

            low = jnp.clip(edges[at_first] - base, 0, tok) // BK
            mid = jnp.clip(edges[at_last] - base + BK - 1, 0, tok) // BK
            mid = jnp.maximum(low, mid)
            total = lax.fori_loop(low, mid, functools.partial(body, masked=True), total)
            total = lax.fori_loop(mid, n_keys, functools.partial(body, masked=False), total)
        rounded = total.astype(BF)
        mixed[rows, :] = rounded
        for k in range(n):
            pieces[k][rows, :] = nn(rounded, wo[:, tiles(share, order[k])]).astype(BF)


def tile_back(bias, q_tile, g_tile, k_tile, v_tile, keep, g_query, rows, sums):
    s = sigmoid_of(nt(k_tile, q_tile), bias)
    g_weight = nt(v_tile, g_tile)
    if keep is not None:
        s = jnp.where(keep, s, 0.0)
    g_s = (g_weight * (s * (1.0 - s))).astype(BF)
    g_value = sums[1] + nn(s.astype(BF), g_tile)
    g_key = sums[0] + nn(g_s, q_tile)
    g_query[rows, :] = g_query[rows, :] + tn(g_s, k_tile)
    return g_key, g_value


def count_tiles(edges, n_q, which, limit):
    return sum([(edges[which + 2 * i] <= limit).astype(I32) for i in range(n_q)], jnp.int32(0))


def far_back_kernel(bias, tok, n_far, edges, start, q, g, *refs):
    kvs, g_query, outs = refs[:n_far], refs[n_far], refs[n_far + 1 :]
    n_q = tok // BQ
    g_query[...] = jnp.zeros_like(g_query)
    for i in reversed(range(n_far)):
        base = edges[0] - (i + 1) * tok
        kv, out = kvs[i], outs[i]

        def key_tile(ki, carry):
            at = tiles(BK, ki)
            k_tile, v_tile = kv[at, :HDIM], kv[at, HDIM:]
            key0 = base + ki * BK
            high = count_tiles(edges, n_q, 1, key0 + BK - 1)
            mid = count_tiles(edges, n_q, 2, key0)

            def body(qi, sums, masked):
                r = tiles(BQ, qi)
                keep = None
                if masked:
                    keep = key0 + lax.broadcasted_iota(I32, (BK, BQ), 0) >= start[:, r]
                return tile_back(bias, q[r, :], g[r, :], k_tile, v_tile, keep, g_query, r, sums)

            zero = jnp.zeros((BK, HDIM), F32)
            sums = lax.fori_loop(0, mid, functools.partial(body, masked=False), (zero, zero))
            g_key, g_value = lax.fori_loop(mid, high, functools.partial(body, masked=True), sums)
            out[at, :HDIM] = (g_key * SCALE).astype(BF)
            out[at, HDIM:] = g_value.astype(BF)
            return carry

        live = jnp.logical_and(base >= 0, edges[1] <= base + tok - 1)

        @pl.when(live)
        def _():
            lax.fori_loop(0, tok // BK, key_tile, 0)

        @pl.when(jnp.logical_not(live))
        def _():
            out[...] = jnp.zeros_like(out)


def own_back_kernel(bias, tok, edges, start, q, g, kv, g_query_in, g_query, out):
    n_q = tok // BQ
    base = edges[0]
    g_query[...] = g_query_in[...]
    for ki in range(tok // BK):
        at = slice(ki * BK, (ki + 1) * BK)
        k_tile, v_tile = kv[at, :HDIM], kv[at, HDIM:]
        key0 = base + ki * BK

        def body(qi, sums):
            r = tiles(BQ, qi)
            k_index = key0 + lax.broadcasted_iota(I32, (BK, BQ), 0)
            q_index = base + qi * BQ + lax.broadcasted_iota(I32, (1, BQ), 1)
            keep = (k_index >= start[:, r]) & (k_index <= q_index)
            return tile_back(bias, q[r, :], g[r, :], k_tile, v_tile, keep, g_query, r, sums)

        zero = jnp.zeros((BK, HDIM), F32)
        high = count_tiles(edges, n_q, 1, key0 + BK - 1)
        g_key, g_value = lax.fori_loop((ki * BK) // BQ, high, body, (zero, zero))
        out[at, :HDIM] = g_key * SCALE
        out[at, HDIM:] = g_value


def call_own(bias, edges, start, q, kv):
    tok = q.shape[0]
    return pl.pallas_call(
        functools.partial(own_kernel, bias, tok),
        out_shape=shape((tok, HDIM), F32),
        in_specs=[SM, VM, VM, VM],
        out_specs=VM,
        compiler_params=params(),
        cost_estimate=cost(16 * tok * tok * HDIM, 4 * tok * HDIM),
        name="attend_own",
    )(edges, start, q, kv)


def call_far(bias, tok, c, rows, edges, order, start, q, acc, wo, kvs):
    n = order.shape[0]

    def part(w):
        return pl.BlockSpec((rows, w), lambda i: (c, 0))

    def full(a):
        return pl.BlockSpec(a.shape, lambda i: (0, 0))

    out = pl.BlockSpec((rows, HDIM), lambda i: (0, 0))
    share = wo.shape[1] // n
    return pl.pallas_call(
        functools.partial(far_kernel, bias, tok, c * rows, len(kvs), n),
        grid=(1,),
        out_shape=[shape((rows, HDIM), BF)] + [shape((rows, share), BF)] * n,
        in_specs=[SM, SM, part(1), part(HDIM), part(HDIM), full(wo)] + [full(a) for a in kvs],
        out_specs=[out] + [pl.BlockSpec((rows, share), lambda i: (0, 0))] * n,
        compiler_params=params(),
        cost_estimate=cost(20 * rows * tok * HDIM + 12 * rows * n * share * HDIM, 4 * rows * n * share),
        name="attend_far",
    )(edges, order, start, q, acc, wo, *kvs)


def call_far_back(bias, edges, start, q, g, kvs):
    tok = q.shape[0]
    return pl.pallas_call(
        functools.partial(far_back_kernel, bias, tok, len(kvs)),
        out_shape=[shape((tok, HDIM), F32)] + [shape((tok, 2 * HDIM), BF)] * len(kvs),
        in_specs=[SM] + [VM] * (3 + len(kvs)),
        out_specs=[VM] * (1 + len(kvs)),
        compiler_params=params(),
        cost_estimate=cost(48 * tok * tok * HDIM, 16 * tok * HDIM),
        name="attend_far_back",
    )(edges, start, q, g, *kvs)


def call_own_back(bias, edges, start, q, g, kv, g_query):
    tok = q.shape[0]
    return pl.pallas_call(
        functools.partial(own_back_kernel, bias, tok),
        out_shape=[shape((tok, HDIM), F32), shape((tok, 2 * HDIM), F32)],
        in_specs=[SM] + [VM] * 5,
        out_specs=[VM] * 2,
        compiler_params=params(),
        cost_estimate=cost(28 * tok * tok * HDIM, 16 * tok * HDIM),
        name="attend_own_back",
    )(edges, start, q, g, kv, g_query)


def ffn_kernel(n, order, *refs):
    hs = refs[:n]
    cot, inv_gain, wg, wu, wd, hidden, g_gu, r2_out, m2 = refs[n : n + 9]
    pieces = refs[n + 9 :]
    share, hid = hs[0].shape[1], wg.shape[1]
    squares = gate = up = None
    for k in range(n):
        h = hs[k][...]
        v = h.astype(F32) * inv_gain[pl.ds(order[k], 1), :]
        squares = add(squares, v * v)
        rows = tiles(share, order[k])
        gate = add(gate, nn(h, wg[rows, :]))
        up = add(up, nn(h, wu[rows, :]))
    r2 = lax.rsqrt(jnp.sum(squares, axis=-1, keepdims=True) / (n * share) + EPS)
    g_hidden = nt(cot[...], wd[...])
    gate = gate * r2
    up = up * r2
    sig = jax.nn.sigmoid(gate)
    silu = gate * sig
    hidden[...] = (silu * up).astype(BF)
    g_gate = g_hidden * up * sig * (1.0 + gate * (1.0 - sig))
    g_up = g_hidden * silu
    m2[...] = row_sums(g_gate * gate + g_up * up)
    g_gate = (g_gate * r2).astype(BF)
    g_up = (g_up * r2).astype(BF)
    g_gu[:, :hid] = g_gate
    g_gu[:, hid:] = g_up
    r2_out[...] = jnp.broadcast_to(r2, r2_out.shape)
    for k in range(n):
        rows = tiles(share, order[k])
        pieces[k][...] = (nt(g_gate, wg[rows, :]) + nt(g_up, wu[rows, :])).astype(BF)


def call_ffn(order, c, hs, cot, inv_gain, wg, wu, wd):
    n = len(hs)
    rows, share = hs[0].shape
    hid = wg.shape[1]
    bt = min(rows, 256)
    steps = rows // bt

    def row(w, skip=0):
        return pl.BlockSpec((bt, w), lambda i, o: (i + skip, 0))

    def full(a):
        return pl.BlockSpec(a.shape, lambda i, o: (0, 0))

    spec = pltpu.PrefetchScalarGridSpec(
        num_scalar_prefetch=1,
        grid=(steps,),
        in_specs=[row(share)] * n
        + [row(n * share, c * steps)]
        + [full(a) for a in (inv_gain, wg, wu, wd)],
        out_specs=[row(hid), row(2 * hid), row(128), pl.BlockSpec((8, bt), lambda i, o: (0, i))]
        + [row(share)] * n,
    )
    return pl.pallas_call(
        functools.partial(ffn_kernel, n),
        grid_spec=spec,
        out_shape=[
            shape((rows, hid), BF),
            shape((rows, 2 * hid), BF),
            shape((rows, 128), F32),
            shape((8, rows), F32),
        ]
        + [shape((rows, share), BF)] * n,
        compiler_params=params(),
        cost_estimate=cost(2 * 5 * rows * n * share * hid, 14 * rows * n * share),
        name="ffn",
    )(order, *hs, cot, inv_gain, wg, wu, wd)


def down_kernel(n, order, hidden, wd, *pieces):
    share = wd.shape[1] // n
    for k in range(n):
        pieces[k][...] = nn(hidden[...], wd[:, tiles(share, order[k])]).astype(BF)


def call_down(order, hidden, wd):
    n = order.shape[0]
    rows, share = hidden.shape[0], wd.shape[1] // n
    return pl.pallas_call(
        functools.partial(down_kernel, n),
        out_shape=[shape((rows, share), BF)] * n,
        in_specs=[SM, VM, VM],
        out_specs=[VM] * n,
        compiler_params=params(),
        cost_estimate=cost(3 * rows * n * share * hidden.shape[1], 4 * rows * n * share),
        name="down",
    )(order, hidden, wd)


def g_mixed_kernel(n, order, wo, *refs):
    rights, g_mixed = refs[:-1], refs[-1]
    rows, share = rights[0].shape
    for c in range(len(rights) // n):
        total = None
        for k in range(n):
            total = add(total, nt(rights[c * n + k][...], wo[:, tiles(share, order[k])]))
        g_mixed[c * rows : (c + 1) * rows, :] = total.astype(BF)


def call_g_mixed(order, wo, rights):
    n = order.shape[0]
    tok = rights[0].shape[0] * len(rights) // n
    return pl.pallas_call(
        functools.partial(g_mixed_kernel, n),
        out_shape=shape((tok, wo.shape[0]), BF),
        in_specs=[SM, VM] + [VM] * len(rights),
        out_specs=VM,
        compiler_params=params(),
        cost_estimate=cost(5 * tok * wo.shape[0] * wo.shape[1], 4 * tok * wo.shape[1]),
        name="g_mixed",
    )(order, wo, *rights)


def gate_grad_kernel(n, chunks, order, *refs):
    lefts, gs, out_g, out_u = refs[: n * chunks], refs[n * chunks : -2], refs[-2], refs[-1]
    share, hid = lefts[0].shape[1], out_g.shape[1]
    for k in range(n):
        total = None
        for c in range(chunks):
            total = add(total, tn(lefts[c * n + k][...], gs[c][...]))
        rows = tiles(share, order[k])
        out_g[rows, :] = total[:, :hid].astype(BF)
        out_u[rows, :] = total[:, hid:].astype(BF)


def call_gate_grad(order, lefts, gs):
    n, chunks = order.shape[0], len(gs)
    dims = (n * lefts[0].shape[1], gs[0].shape[1] // 2)
    return pl.pallas_call(
        functools.partial(gate_grad_kernel, n, chunks),
        out_shape=[shape(dims, BF)] * 2,
        in_specs=[SM] + [VM] * (len(lefts) + chunks),
        out_specs=[VM, VM],
        compiler_params=params(),
        cost_estimate=cost(2 * chunks * gs[0].shape[0] * gs[0].shape[1] * dims[0], 4 * chunks * gs[0].shape[0] * dims[0]),
        name="grad_gate_up",
    )(order, *lefts, *gs)


def down_grad_kernel(n, per, order, cot, *refs):
    hiddens, out = refs[:-1], refs[-1]
    share, (rows, hid) = cot.shape[1] // n, hiddens[0].shape
    for k in range(n):
        total = None
        for c, hidden in enumerate(hiddens):
            total = add(total, tn(hidden[...], cot[c * rows : (c + 1) * rows, k * share : (k + 1) * share]))
        at, col = (k // per) * hid, (k % per) * share
        out[at : at + hid, col : col + share] = total.astype(BF)


def call_down_grad(order, per, cot, hiddens):
    n = order.shape[0]
    share, hid = cot.shape[1] // n, hiddens[0].shape[1]
    return pl.pallas_call(
        functools.partial(down_grad_kernel, n, per),
        out_shape=shape((n // per * hid, per * share), BF),
        in_specs=[SM, VM] + [VM] * len(hiddens),
        out_specs=VM,
        compiler_params=params(),
        cost_estimate=cost(3 * cot.shape[0] * cot.shape[1] * hid, 4 * cot.shape[0] * cot.shape[1]),
        name="grad_down",
    )(order, cot, *hiddens)


def qkv_back_kernel(n, n_far, order, g_query, g_kv, q, kv, cos, sin, wq, wk, wv, *refs):
    arrived, g_qkv, m1, pieces = refs[:n_far], refs[n_far], refs[n_far + 1], refs[n_far + 2 :]
    share = wq.shape[0] // n
    total = g_kv[...]
    for a in arrived:
        total = total + a[...].astype(F32)
    gq, gk, gv = g_query[...] * SCALE, total[:, :HDIM], total[:, HDIM:]
    m1[...] = row_sums(
        gq * q[...].astype(F32) + gk * kv[:, :HDIM].astype(F32) + gv * kv[:, HDIM:].astype(F32)
    )
    c, s = cos[...], sin[...]

    def back(v):
        return (v * c - pltpu.roll(v, HDIM // 2, 1) * s).astype(BF)

    gq, gk, gv = back(gq), back(gk), gv.astype(BF)
    g_qkv[:, :HDIM] = gq
    g_qkv[:, HDIM : 2 * HDIM] = gk
    g_qkv[:, 2 * HDIM :] = gv
    for k in range(n):
        rows = tiles(share, order[k])
        pieces[k][...] = (nt(gq, wq[rows, :]) + nt(gk, wk[rows, :]) + nt(gv, wv[rows, :])).astype(BF)


def call_qkv_back(order, g_query, g_kv, q, kv, cos, sin, wq, wk, wv, arrived):
    n, n_far = order.shape[0], len(arrived)
    tok = q.shape[0]
    bt = min(tok, 256)

    def row(w):
        return pl.BlockSpec((bt, w), lambda i, o: (i, 0))

    def full(a):
        return pl.BlockSpec(a.shape, lambda i, o: (0, 0))

    share = wq.shape[0] // n
    spec = pltpu.PrefetchScalarGridSpec(
        num_scalar_prefetch=1,
        grid=(tok // bt,),
        in_specs=[row(HDIM), row(2 * HDIM), row(HDIM), row(2 * HDIM), row(HDIM), row(HDIM)]
        + [full(a) for a in (wq, wk, wv)]
        + [row(2 * HDIM)] * n_far,
        out_specs=[row(3 * HDIM), pl.BlockSpec((8, bt), lambda i, o: (0, i))] + [row(share)] * n,
    )
    return pl.pallas_call(
        functools.partial(qkv_back_kernel, n, n_far),
        grid_spec=spec,
        out_shape=[shape((tok, 3 * HDIM), BF), shape((8, tok), F32)] + [shape((tok, share), BF)] * n,
        compiler_params=params(),
        cost_estimate=cost(6 * tok * n * share * 3 * HDIM, 4 * tok * n * share),
        name="qkv_back",
    )(order, g_query, g_kv, q, kv, cos, sin, wq, wk, wv, *arrived)


def tail_grad_kernel(n, chunks, order, left, g_qkv, *refs):
    mixed, rights, out = refs[:chunks], refs[chunks:-1], refs[-1]
    share, rows = left.shape[1] // n, mixed[0].shape[0]
    for k in range(n):
        at = tiles(share, order[k])
        out[at, : 3 * HDIM] = tn(left[:, k * share : (k + 1) * share], g_qkv[...]).astype(BF)
        total = None
        for c in range(chunks):
            total = add(total, tn(rights[c * n + k][...], mixed[c][...]))
        out[at, 3 * HDIM :] = total.astype(BF)


def call_tail_grad(order, left, g_qkv, mixed, rights):
    n, chunks = order.shape[0], len(mixed)
    return pl.pallas_call(
        functools.partial(tail_grad_kernel, n, chunks),
        out_shape=shape((left.shape[1], 4 * HDIM), BF),
        in_specs=[SM] + [VM] * (2 + chunks + len(rights)),
        out_specs=VM,
        compiler_params=params(),
        cost_estimate=cost(4 * left.shape[0] * left.shape[1] * 4 * HDIM, 4 * left.shape[0] * left.shape[1]),
        name="grad_tail",
    )(order, left, g_qkv, *mixed, *rights)


def folded(n):
    return [0] + list(range(1, n, 2)) + list(range(n - 2 + n % 2, 0, -2))


class Tp:
    def __init__(self, n_tp):
        self.n = n_tp
        self.pairs = n_tp // 2
        ring = folded(self.pairs)
        place = [ring.index(z) for z in range(self.pairs)]
        self.core_perm = [(i, i ^ 1) for i in range(n_tp)]
        self.ring_to = []
        order = []
        for i in range(n_tp):
            z, c = divmod(i, 2)
            self.ring_to.append(ring[(place[z] + 1) % self.pairs] * 2 + c)
            sources = [ring[(place[z] - j) % self.pairs] * 2 for j in range(self.pairs)]
            order.append([s + (c ^ b) for s in sources for b in (0, 1)])
        self.order = jnp.asarray(order, I32)[lax.axis_index("tp")]

    def core(self, a):
        return lax.ppermute(a, "tp", self.core_perm)

    def step(self, a, distance=1):
        perm = []
        for i in range(self.n):
            j = i
            for _ in range(distance):
                j = self.ring_to[j]
            perm.append((i, j))
        return lax.ppermute(a, "tp", perm)

    def gather(self, block, work=()):
        got, cur = [], block
        for j in range(self.pairs):
            if j == 2:
                cur = after(cur, *work)
            if j:
                cur = self.step(cur)
            got += [cur, self.core(cur)]
        return got

    def scatter(self, pieces, small=None, work=()):
        if small is not None:
            small = small + self.core(small)
            small = sum([self.step(small, d) for d in range(1, self.pairs)], small)
        acc, held, done = None, (), []
        for hop, j in enumerate(list(range(1, self.pairs)) + [0]):
            term = pieces[2 * j].astype(F32) + self.core(pieces[2 * j + 1]).astype(F32)
            if hop:
                acc = acc.astype(BF)
                if hop == 2 and small is not None:
                    acc, small = lax.optimization_barrier((acc, small))
                acc = after(acc, *held)
                held = ()
                if hop <= len(work):
                    held = work[hop - 1](acc)
                    done += held
                term = term + self.step(acc).astype(F32)
            acc = term
        if held:
            acc = after(acc, *held)
        return (acc, small, *done)


def after(value, *others):
    return lax.optimization_barrier((value, *others))[0]


def sum_ctx(a, n_ctx, rank):
    if n_ctx != 4:
        return lax.psum(a, "ctx")

    def halves(a, bit):
        half = a.shape[0] // 2
        keep = lax.dynamic_slice_in_dim(a, bit * half, half, 0)
        give = lax.dynamic_slice_in_dim(a, (1 - bit) * half, half, 0)
        return keep, give

    def swap(a, mask):
        return lax.ppermute(a, "ctx", [(r, r ^ mask) for r in range(4)])

    def joined(mine, got, bit):
        return jnp.where(bit == 0, jnp.concatenate([mine, got], 0), jnp.concatenate([got, mine], 0))

    bits = (rank % 2, rank // 2)
    rows = a.shape[0] // 2
    parts = []
    for part, first in ((a[:rows], 0), (a[rows:], 1)):
        for axis in (first, 1 - first):
            keep, give = halves(part, bits[axis])
            part = (keep.astype(F32) + swap(give, 1 << axis).astype(F32)).astype(BF)
        for axis in (1 - first, first):
            part = joined(part, swap(part, 1 << axis), bits[axis])
        parts.append(part)
    return jnp.concatenate(parts, axis=0)


def per_device(
    layer_in,
    gain_attn,
    gain_ffn,
    w_query,
    w_key,
    w_value,
    w_out,
    w_gate,
    w_up,
    w_down,
    doc_ids,
    positions,
    cotangent,
):
    tok, share = layer_in.shape
    n_ctx, n_tp = lax.axis_size("ctx"), lax.axis_size("tp")
    width = share * n_tp
    tp = Tp(n_tp)
    order = tp.order
    rank = lax.axis_index("ctx").astype(I32)
    own = lax.axis_index("tp") * share
    bias = -math.log(tok * n_ctx)
    rows = tok // CHUNKS
    parts = [slice(c * rows, (c + 1) * rows) for c in range(CHUNKS)]
    gain_a_own = lax.dynamic_slice_in_dim(gain_attn, own, share, 0)
    gain_f_own = lax.dynamic_slice_in_dim(gain_ffn, own, share, 0)

    def shift(a, s):
        return lax.ppermute(a, "ctx", [(r, r + s) for r in range(n_ctx) if 0 <= r + s < n_ctx])

    def broad(a):
        return jnp.tile(a, (1, share // a.shape[1]))

    per = max(1, min(4 * HDIM // share, n_tp))

    freq = THETA ** (-(jnp.arange(HDIM // 2, dtype=F32) * 2.0 / HDIM))
    angle = positions.astype(F32)[:, None] * freq[None, :]
    cos, sin = jnp.cos(angle), jnp.sin(angle)
    cos, sin = jnp.concatenate([cos, cos], 1), jnp.concatenate([-sin, sin], 1)
    q_start = rank * tok + jnp.arange(tok, dtype=I32) - positions
    edges = edges_of(rank, tok, q_start)
    gain_blocks, inv_gain = gain_attn.reshape(n_tp, share), (1.0 / gain_ffn).reshape(n_tp, share)
    start_col, start_row = q_start[:, None], q_start[None, :]
    prepared = lax.optimization_barrier((cos, sin, edges, start_col, start_row, gain_blocks, inv_gain, order))
    cos, sin, edges, start_col, start_row, gain_blocks, inv_gain, order = prepared
    xs = tp.gather(layer_in, prepared)
    normed, q_rot, kv_own, r1 = call_qkv(order, xs, gain_blocks, w_query, w_key, w_value, cos, sin)
    cot_full = lax.all_gather(after(cotangent, xs[-2]), "tp", axis=1, tiled=True)
    kv_far = [shift(kv_own, s) for s in range(1, n_ctx)]
    acc = call_own(bias, edges, start_col, q_rot, kv_own)
    mixed, hs, h_own = [], [], []
    for c, part in enumerate(parts):
        out, *pieces = call_far(bias, tok, c, rows, edges, order, start_col, q_rot, acc, w_out, kv_far)
        mixed.append(out)
        h = layer_in[part].astype(F32) + tp.scatter(pieces)[0]
        h_own.append(h)
        hs.append(tp.gather((h * gain_f_own).astype(BF)))

    hiddens, g_gus, g_hs, g_hbs = [], [], [], []
    grad_gain_two = 0.0
    for c, part in enumerate(parts):
        hidden, g_gu, r2, m2, *pieces = call_ffn(order, c, hs[c], cot_full, inv_gain, w_gate, w_up, w_down)
        hiddens.append(hidden)
        g_gus.append(g_gu)
        work = ()
        if c == CHUNKS - 1:

            def grads_1(sent):
                return call_gate_grad(order, sum(hs, []), [after(g, sent) for g in g_gus])

            def grads_2(sent):
                return [call_down_grad(order, per, after(cot_full, sent), hiddens)]

            work = (grads_1, grads_2)
        dn2, m2, *grads = tp.scatter(pieces, m2[0], work)
        m2 = m2 / width
        r2 = broad(r2)
        g_h = cotangent[part].astype(F32) + gain_f_own * dn2 - (r2 * r2 * m2[:, None]) * h_own[c]
        grad_gain_two = grad_gain_two + jnp.sum(dn2 * h_own[c], axis=0)
        g_hs.append(g_h)
        g_hbs.append(tp.gather(g_h.astype(BF)))

    hidden = jnp.concatenate(hiddens, 0)
    grad_gate, grad_up, grad_down = lax.psum(tuple(grads), "ctx")
    down = call_down(order, hidden, w_down)
    g_hbs[-1][-2], *down = lax.optimization_barrier((g_hbs[-1][-2], *down))
    g_mixed = call_g_mixed(order, w_out, sum(g_hbs, []))
    g_query, *g_kv_far = call_far_back(bias, edges, start_row, q_rot, g_mixed, kv_far)
    arrived = [shift(g, -s) for s, g in zip(range(1, n_ctx), g_kv_far)]
    g_query, g_kv = call_own_back(bias, edges, start_row, q_rot, g_mixed, kv_own, g_query)
    down = tp.scatter(down)[0]
    outs = (jnp.concatenate(h_own, 0) + down).astype(BF)
    g_kv = after(g_kv, outs, grad_gate, grad_up, grad_down)
    g_qkv, m1, *pieces = call_qkv_back(
        order, g_query, g_kv, q_rot, kv_own, cos, sin, w_query, w_key, w_value, arrived
    )

    def grads_3(sent):
        return [call_tail_grad(order, normed, after(g_qkv, sent), mixed, sum(g_hbs, []))]

    dn1, m1, tail = tp.scatter(pieces, m1[0], (grads_3,))
    m1 = m1 / width
    r1 = broad(r1)
    x_hat = layer_in.astype(F32) * r1
    g_input = jnp.concatenate(g_hs, 0) + r1 * (dn1 * gain_a_own - x_hat * m1[:, None])
    grad_gain_one = jnp.sum(dn1 * x_hat, axis=0)

    tail = sum_ctx(tail, n_ctx, rank).astype(F32)
    hid = w_gate.shape[1]
    down_blocks = [grad_down[i * hid : (i + 1) * hid] for i in range(n_tp // per)]
    gains = jnp.concatenate([grad_gain_one, grad_gain_two])
    gains = sum(
        [lax.ppermute(gains, "ctx", [(r, (r + s) % n_ctx) for r in range(n_ctx)]) for s in range(1, n_ctx)],
        gains,
    )
    return (
        outs,
        g_input,
        gains[:share],
        gains[share:],
        tail[:, :HDIM],
        tail[:, HDIM : 2 * HDIM],
        tail[:, 2 * HDIM : 3 * HDIM],
        tail[:, 3 * HDIM :].T,
        grad_gate.astype(F32),
        grad_up.astype(F32),
        jnp.concatenate(down_blocks, 1).astype(F32),
    )


def solution(mesh):
    row, col = P("tp", None), P(None, "tp")
    both = P("ctx", "tp")
    in_specs = (both, P(), P(), col, col, col, row, col, col, row, P("ctx"), P("ctx"), both)
    out_specs = (both, both, P("tp"), P("tp"), col, col, col, row, col, col, row)
    return jax.shard_map(
        per_device, mesh=mesh, in_specs=in_specs, out_specs=out_specs, check_vma=False
    )
```

time: 684 us -> 506 us (0.74)
  waiting for transfers between devices: 384 us -> 290 us
  Pallas kernels: 0 us -> 91.3 us
  matrix products: 75.5 us -> 0 us
  local copies, waits for them, and re-layouts: 80.9 us -> 18 us
  blocking collectives: 18 us -> 0 us
  between operations: 26.6 us -> 15.2 us
  other arithmetic: 40.1 us -> 33 us
    pallas_call x0 -> x12, Pallas kernels: none -> 91.3 us  [the longest x1 20 us: call_ffn(): pl.pallas_call(functools.partial(ffn_kernel, n), grid_spec=spec, out_shap...]
    dot_general x24 -> x0, matrix products: 75.5 us -> none  [the longest x12 60 us: dot(): lax.dot_general(a, b, (dims, ((), ())), preferred_element_type=F32)]
    ppermute x6, waiting for transfers between devices: 79.4 us -> 14 us  [shift(): lax.ppermute(a, 'ctx', [(r, r + s) for r in range(n_ctx) if 0 <= r + s <...]
    unnamed x181 -> x83, local copies, waits for them, and re-layouts: 48.8 us -> 5.52 us
    ppermute x30 -> x38, waiting for transfers between devices: 237 us -> 207 us  [the longest x27 184 us: step(): return lax.ppermute(a, 'tp', perm)]
    psum x1 -> x0, blocking collectives: 18 us -> none  [per_device(): gains = lax.psum(jnp.concatenate([grad_gain_one, grad_gain_two]), 'ctx')]
    convert_element_type x15 -> x23, other arithmetic: 9.23 us -> 24.7 us  [the longest x12 10.8 us: scatter(): acc = acc.astype(BF)]
    dynamic_slice x15 -> x5, local copies, waits for them, and re-layouts: 13.4 us -> 0.89 us  [the longest x1 0.76 us: per_device(): gain_f_own = lax.dynamic_slice_in_dim(gain_ffn, own, share, 0)]
  transfers between devices with their start and end apart: 71 -> 76, of which waited for: 33 -> 34; matrix products, arithmetic and copies ran while one was open for 17% -> 9% of each run, Pallas kernels for 0% -> 13%
where the time goes in v2:
time: 506 us; the launch traced here: 497 us
  waiting for transfers between devices  290 us (57%)
  Pallas kernels  91.3 us (18%)
  starting transfers between devices  49.7 us (10%)
  other arithmetic  33 us (7%)
  local copies, waits for them, and re-layouts  18 us (4%)
  between operations  15.2 us (3%)
    ppermute x27, waiting for transfers between devices, step(): return lax.ppermute(a, 'tp', perm)  184 us
    psum x1, waiting for transfers between devices, per_device(): grad_gate, grad_up, grad_down = lax.psum(tuple(grads), 'ctx')  62.2 us
    ppermute x8, waiting for transfers between devices, swap(): return lax.ppermute(a, 'ctx', [(r, r ^ mask) for r in range(4)])  22.7 us
    ppermute x27, starting transfers between devices, step(): return lax.ppermute(a, 'tp', perm)  22.5 us
    pallas_call x1, Pallas kernels, call_ffn(): pl.pallas_call(functools.partial(ffn_kernel, n), grid_spec=spec, out_shap...  20 us
    ppermute x6, waiting for transfers between devices, shift(): lax.ppermute(a, 'ctx', [(r, r + s) for r in range(n_ctx) if 0 <= r + s <...  14 us
    ppermute x6, starting transfers between devices, shift(): lax.ppermute(a, 'ctx', [(r, r + s) for r in range(n_ctx) if 0 <= r + s <...  11.4 us
    convert_element_type x12, other arithmetic, scatter(): acc = acc.astype(BF)  10.8 us
  transfers between devices with their start and end apart: 76, of which 34 were waited for; matrix products, arithmetic and copies ran while one was open for 9% of the time, Pallas kernels for 13%

profile of v2, /device:TPU:0, one launch (start us, length us, event | category | flops | bytes accessed | tf_op | source)
XLA Modules:
  0.0 496.8 jit_solution(13736047123193977981)
XLA Ops:
  24.4 13.1 %collective-permute-done.3.refs_4_ = bf16[1024,256]{1,0:T(8,128)(2,1)S(1)} collective-permute-done((bf16[1024,256]{1,0:T(8,128)(2,1)S(1)}, bf16[1024,256]{1,0:T(8,128)(2,1)S(1)}, u32[]{:S(2)}, u32[]{:S(2)}) %collective-permute-start.3) | collective-permute-done | bytes 524320 | tf_op jit(solution)/shard_map/ppermute | solution.py:604
  38.5 12.1 %collective-permute-done.5.refs_6_ = bf16[1024,256]{1,0:T(8,128)(2,1)S(1)} collective-permute-done((bf16[1024,256]{1,0:T(8,128)(2,1)S(1)}, bf16[1024,256]{1,0:T(8,128)(2,1)S(1)}, u32[]{:S(2)}, u32[]{:S(2)}) %collective-permute-start.5) | collective-permute-done | bytes 524320 | tf_op jit(solution)/shard_map/ppermute | solution.py:604
  52.6 9.7 %norm_qkv.1 = (bf16[1024,2048]{1,0:T(8,128)(2,1)}, bf16[1024,128]{1,0:T(8,128)(2,1)}, bf16[1024,256]{1,0:T(8,128)(2,1)}, f32[1024,128]{1,0:T(8,128)}) custom-call(s32[8]{0:T(128)} %fusion.4.order, bf16[1024,256]{1,0:T(8,128)(2,1)} %refs_0_.1, bf16[1024,256]{1,0:T(8,128)(2,1)} %copy-done.40, bf16[1024,256]{1,0:T(8,128)(2,1)} %copy-done.34, ...), custom_call_target="tpu_custom_call" | custom-call | flops 10737418240 | bytes 20971520 | tf_op jit(solution)/shard_map/norm_qkv/pallas_call | solution.py:111
  77.7 11.3 %collective-permute-done.8.refs_1_ = bf16[1024,256]{1,0:T(8,128)(2,1)S(1)} collective-permute-done((bf16[1024,256]{1,0:T(8,128)(2,1)}, bf16[1024,256]{1,0:T(8,128)(2,1)S(1)}, u32[]{:S(2)}, u32[]{:S(2)}) %collective-permute-start.8) | collective-permute-done | bytes 524320 | tf_op jit(solution)/shard_map/ppermute | solution.py:701
  100.5 14.1 %collective-permute-done.14 = bf16[1024,256]{1,0:T(8,128)(2,1)S(1)} collective-permute-done((bf16[1024,256]{1,0:T(8,128)(2,1)S(1)}, bf16[1024,256]{1,0:T(8,128)(2,1)S(1)}, u32[]{:S(2)}, u32[]{:S(2)}) %collective-permute-start.14) | collective-permute-done | bytes 524320 | tf_op jit(solution)/shard_map/ppermute | solution.py:604
  116.8 13.3 %collective-permute-done.15 = bf16[1024,256]{1,0:T(8,128)(2,1)S(1)} collective-permute-done((bf16[1024,256]{1,0:T(8,128)(2,1)S(1)}, bf16[1024,256]{1,0:T(8,128)(2,1)S(1)}, u32[]{:S(2)}, u32[]{:S(2)}) %collective-permute-start.15) | collective-permute-done | bytes 524320 | tf_op jit(solution)/shard_map/ppermute | solution.py:604
  131.8 11.7 %collective-permute-done.16 = bf16[1024,256]{1,0:T(8,128)(2,1)} collective-permute-done((bf16[1024,256]{1,0:T(8,128)(2,1)S(1)}, bf16[1024,256]{1,0:T(8,128)(2,1)}, u32[]{:S(2)}, u32[]{:S(2)}) %collective-permute-start.16) | collective-permute-done | bytes 524320 | tf_op jit(solution)/shard_map/ppermute | solution.py:604
  145.6 11.5 %collective-permute-done.18.refs_2_ = bf16[1024,256]{1,0:T(8,128)(2,1)S(1)} collective-permute-done((bf16[1024,256]{1,0:T(8,128)(2,1)S(1)}, bf16[1024,256]{1,0:T(8,128)(2,1)S(1)}, u32[]{:S(2)}, u32[]{:S(2)}) %collective-permute-start.18) | collective-permute-done | bytes 524320 | tf_op jit(solution)/shard_map/ppermute | solution.py:604
  157.9 11.3 %collective-permute-done.20.refs_4_ = bf16[1024,256]{1,0:T(8,128)(2,1)S(1)} collective-permute-done((bf16[1024,256]{1,0:T(8,128)(2,1)S(1)}, bf16[1024,256]{1,0:T(8,128)(2,1)S(1)}, u32[]{:S(2)}, u32[]{:S(2)}) %collective-permute-start.20) | collective-permute-done | bytes 524320 | tf_op jit(solution)/shard_map/ppermute | solution.py:604
  170.5 9.1 %collective-permute-done.22.refs_6_ = bf16[1024,256]{1,0:T(8,128)(2,1)S(1)} collective-permute-done((bf16[1024,256]{1,0:T(8,128)(2,1)S(1)}, bf16[1024,256]{1,0:T(8,128)(2,1)S(1)}, u32[]{:S(2)}, u32[]{:S(2)}) %collective-permute-start.22) | collective-permute-done | bytes 524320 | tf_op jit(solution)/shard_map/ppermute | solution.py:604
  181.7 20.0 %ffn.1 = (bf16[1024,512]{1,0:T(8,128)(2,1)}, bf16[1024,1024]{1,0:T(8,128)(2,1)}, f32[1024,128]{1,0:T(8,128)}, f32[8,1024]{1,0:T(8,128)}, bf16[1024,256]{1,0:T(8,...) custom-call(s32[8]{0:T(128)} %fusion.4.order, ...), custom_call_target="tpu_custom_call" | custom-call | flops 21474836480 | bytes 29360128 | tf_op jit(solution)/shard_map/ffn/pallas_call | solution.py:384
  213.7 9.2 %grad_gate_up.1 = (bf16[2048,512]{1,0:T(8,128)(2,1)}, bf16[2048,512]{1,0:T(8,128)(2,1)}) custom-call(s32[8]{0:T(128)} %fusion.4.order, bf16[1024,256]{1,0:T(8,128)(2,1)} %copy-done.16, bf16[1024,256]{1,0:T(8,128)(2,1)} %copy-done.35, bf16[1024,256]{1,0:T(8,128)(2,1)} %copy-done.30, bf16[1024,256]{1,0:T(8,128)(2,1)} %copy-done.36, ...), custom_call_target="tpu_custom_call" | custom-call | flops 8589934592 | bytes 8388608 | tf_op jit(solution)/shard_map/grad_gate_up/pallas_call | solution.py:459
  234.8 7.1 %collective-permute-done.33 = bf16[1024,256]{1,0:T(8,128)(2,1)S(1)} collective-permute-done((bf16[1024,256]{1,0:T(8,128)(2,1)}, bf16[1024,256]{1,0:T(8,128)(2,1)S(1)}, u32[]{:S(2)}, u32[]{:S(2)}) %collective-permute-start.33) | collective-permute-done | bytes 524320 | tf_op jit(solution)/shard_map/ppermute | solution.py:604
  243.0 12.4 %collective-permute-done.34 = bf16[1024,256]{1,0:T(8,128)(2,1)} collective-permute-done((bf16[1024,256]{1,0:T(8,128)(2,1)}, bf16[1024,256]{1,0:T(8,128)(2,1)}, u32[]{:S(2)}, u32[]{:S(2)}) %collective-permute-start.34) | collective-permute-done | bytes 524320 | tf_op jit(solution)/shard_map/ppermute | solution.py:604
  257.8 11.6 %collective-permute-done.35.refs_2_.refs_3_ = bf16[1024,256]{1,0:T(8,128)(2,1)} collective-permute-done((bf16[1024,256]{1,0:T(8,128)(2,1)S(1)}, bf16[1024,256]{1,0:T(8,128)(2,1)}, u32[]{:S(2)}, u32[]{:S(2)}) %collective-permute-start.35) | collective-permute-done | bytes 524320 | tf_op jit(solution)/shard_map/ppermute | solution.py:604
  269.5 12.1 %collective-permute-done.36.refs_4_.refs_5_ = bf16[1024,256]{1,0:T(8,128)(2,1)} collective-permute-done((bf16[1024,256]{1,0:T(8,128)(2,1)}, bf16[1024,256]{1,0:T(8,128)(2,1)}, u32[]{:S(2)}, u32[]{:S(2)}) %collective-permute-start.36) | collective-permute-done | bytes 524320 | tf_op jit(solution)/shard_map/ppermute | solution.py:604
  302.5 8.9 %collective-permute-done.42 = bf16[1024,256]{1,0:T(8,128)(2,1)} collective-permute-done((bf16[1024,256]{1,0:T(8,128)(2,1)S(1)}, bf16[1024,256]{1,0:T(8,128)(2,1)}, u32[]{:S(2)}, u32[]{:S(2)}) %collective-permute-start.42) | collective-permute-done | bytes 524320 | tf_op jit(solution)/shard_map/ppermute | solution.py:604
  319.9 7.3 %collective-permute-done.43 = bf16[1024,256]{1,0:T(8,128)(2,1)S(1)} collective-permute-done((bf16[1024,256]{1,0:T(8,128)(2,1)S(1)}, bf16[1024,256]{1,0:T(8,128)(2,1)S(1)}, u32[]{:S(2)}, u32[]{:S(2)}) %collective-permute-start.43) | collective-permute-done | bytes 524320 | tf_op jit(solution)/shard_map/ppermute | solution.py:604
  329.3 6.6 %attend_own_back.1 = (f32[1024,128]{1,0:T(8,128)}, f32[1024,256]{1,0:T(8,128)}) custom-call(s32[5]{0:T(128)} %pad_add_fusion.1.edges, s32[1,1024]{1,0:T(1,128)} %bitcast.31, bf16[1024,128]{1,0:T(8,128)(2,1)} %get-tuple-element.101.q, bf16[1024,128]{1,0:T(8,128)(2,1)} %g_mixed.1.g, bf16[1024,256]{1,0:T(8,128)(2,1)} %get-tuple-element.102.kv, ...), custom_call_target="tpu_custom_call" | custom-call | flops 7516192768 | bytes 2097152 | tf_op jit(solution)/shard_map/attend_own_back/pallas_call | solution.py:318
  335.9 7.0 %collective-permute-done.44 = bf16[1024,256]{1,0:T(8,128)(2,1)S(1)} collective-permute-done((bf16[1024,256]{1,0:T(8,128)(2,1)}, bf16[1024,256]{1,0:T(8,128)(2,1)S(1)}, u32[]{:S(2)}, u32[]{:S(2)}) %collective-permute-start.44) | collective-permute-done | bytes 524320 | tf_op jit(solution)/shard_map/ppermute | solution.py:604
  345.0 62.2 %all-reduce.3.cloned.1.call-done = (bf16[2048,512]{1,0:T(8,128)(2,1)}, bf16[2048,512]{1,0:T(8,128)(2,1)}, bf16[2048,512]{1,0:T(8,128)(2,1)}) async-done(((bf16[2048,512]{1,0:T(8,128)(2,1)}, bf16[2048,512]{1,0:T(8,128)(2,1)}, bf16[2048,512]{1,0:T(8,128)(2,1)}), (bf16[2048,512]{1,0:T(8,128)(2,1)}, bf16[2048,512]{1,0:T(8,128)(2,1)}, bf16[2048,512]{1,0:T(8,128)(2,1)})) %all-reduce.3.cloned.1.call-update) | async-done | bytes 6291472 | tf_op jit(solution)/shard_map/psum | solution.py:756
  407.2 8.4 %qkv_back.1 = (bf16[1024,384]{1,0:T(8,128)(2,1)}, f32[8,1024]{1,0:T(8,128)}, bf16[1024,256]{1,0:T(8,128)(2,1)}, bf16[1024,256]{1,0:T(8,128)(2,1)}, bf16[1024,256...) custom-call(s32[8]{0:T(128)} %fusion.4.order, ...), custom_call_target="tpu_custom_call" | custom-call | flops 9663676416 | bytes 8388608 | tf_op jit(solution)/shard_map/qkv_back/pallas_call | solution.py:539
  432.0 8.5 %grad_tail.1 = bf16[2048,512]{1,0:T(8,128)(2,1)} custom-call(s32[8]{0:T(128)} %fusion.4.order, bf16[1024,2048]{1,0:T(8,128)(2,1)} %get-tuple-element.167.left, bf16[1024,384]{1,0:T(8,128)(2,1)} %get-tuple-element.169.g_qkv, bf16[1024,128]{1,0:T(8,128)(2,1)} %get-tuple-element.170.refs_0_, bf16[1024,256]{1,0:T(8,128)(2,1)} %copy-done.9, ...), custom_call_target="tpu_custom_call" | custom-call | flops 8589934592 | bytes 8388608 | tf_op jit(solution)/shard_map/grad_tail/pallas_call | solution.py:563
  445.7 11.2 %collective-permute-done.70 = bf16[512,512]{1,0:T(8,128)(2,1)S(1)} collective-permute-done((bf16[512,512]{1,0:T(8,128)(2,1)S(1)}, bf16[512,512]{1,0:T(8,128)(2,1)S(1)}, u32[]{:S(2)}, u32[]{:S(2)}) %collective-permute-start.70) | collective-permute-done | bytes 524320 | tf_op jit(solution)/shard_map/ppermute | solution.py:654
  (290 shorter events, 172.0 us)
Async XLA Ops:
  7.2 174.5 %all-gather.2.cloned.1.call-start = ((), (), s32[]{:S(2)}) async-start(), calls=%async_computation | async-start | bytes 4718592 | tf_op jit(solution)/shard_map/all_gather | solution.py:720
  7.2 16.2 %collective-permute-start.1 = (bf16[1024,256]{1,0:T(8,128)(2,1)}, bf16[1024,256]{1,0:T(8,128)(2,1)S(1)}, u32[]{:S(2)}, u32[]{:S(2)}) collective-permute-start(bf16[1024,256]{1,0:T(8,128)(2,1)} %refs_0_.1), channel_id=1, source_target_pairs={{0,2},{1,3},{2,6},{3,7},{4,0},{5,1},{6,4},{7,5},{8,10},{9,11},{10,... | collective-permute-start | bytes 1572872 | tf_op jit(solution)/shard_map/ppermute | solution.py:604
  50.6 356.6 %all-reduce.3.cloned.1.call-start = ((), (), s32[]{:S(2)}) async-start(), calls=%async_computation.1 | async-start | bytes 12582912 | tf_op jit(solution)/shard_map/psum | solution.py:756
  62.3 15.4 %collective-permute-start.7 = (bf16[1024,256]{1,0:T(8,128)(2,1)}, bf16[1024,256]{1,0:T(8,128)(2,1)S(1)}, u32[]{:S(2)}, u32[]{:S(2)}) collective-permute-start(bf16[1024,256]{1,0:T(8,128)(2,1)} %get-tuple-element.102.kv), channel_id=1, source_target_pairs={{0,8},{8,16},{16,24},{1,9},{9,17},{17,25},{2,10},{10,18},{18,26},{... | collective-permute-start | bytes 1572872 | tf_op jit(solution)/shard_map/ppermute | solution.py:701
  65.1 23.9 %collective-permute-start.8 = (bf16[1024,256]{1,0:T(8,128)(2,1)}, bf16[1024,256]{1,0:T(8,128)(2,1)S(1)}, u32[]{:S(2)}, u32[]{:S(2)}) collective-permute-start(bf16[1024,256]{1,0:T(8,128)(2,1)} %get-tuple-element.102.kv), channel_id=1, source_target_pairs={{0,16},{8,24},{1,17},{9,25},{2,18},{10,26},{3,19},{11,27},{4,20},{... | collective-permute-start | bytes 1572872 | tf_op jit(solution)/shard_map/ppermute | solution.py:701
  68.6 20.5 %collective-permute-start.9 = (bf16[1024,256]{1,0:T(8,128)(2,1)}, bf16[1024,256]{1,0:T(8,128)(2,1)S(1)}, u32[]{:S(2)}, u32[]{:S(2)}) collective-permute-start(bf16[1024,256]{1,0:T(8,128)(2,1)} %get-tuple-element.102.kv), channel_id=1, source_target_pairs={{0,24},{1,25},{2,26},{3,27},{4,28},{5,29},{6,30},{7,31}} | collective-permute-start | bytes 1572872 | tf_op jit(solution)/shard_map/ppermute | solution.py:701
  99.7 14.9 %collective-permute-start.14 = (bf16[1024,256]{1,0:T(8,128)(2,1)S(1)}, bf16[1024,256]{1,0:T(8,128)(2,1)S(1)}, u32[]{:S(2)}, u32[]{:S(2)}) collective-permute-start(bf16[1024,256]{1,0:T(8,128)(2,1)S(1)} %add_convert_fusion.14), channel_id=1, source_target_pairs={{0,2},{1,3},{2,6},{3,7},{4,0},{5,1},{6,4},{7,5},{8,10},{9,11},{10,... | collective-permute-start | bytes 1572872 | tf_op jit(solution)/shard_map/ppermute | solution.py:604
  100.5 16.3 %collective-permute-start.11 = (bf16[1024,256]{1,0:T(8,128)(2,1)}, bf16[1024,256]{1,0:T(8,128)(2,1)S(1)}, u32[]{:S(2)}, u32[]{:S(2)}) collective-permute-start(bf16[1024,256]{1,0:T(8,128)(2,1)} %get-tuple-element.106), channel_id=1, source_target_pairs={{0,1},{1,0},{2,3},{3,2},{4,5},{5,4},{6,7},{7,6},{8,9},{9,8},{10,11... | collective-permute-start | bytes 1572872 | tf_op jit(solution)/shard_map/ppermute | solution.py:595
  116.8 15.0 %collective-permute-start.10 = (bf16[1024,256]{1,0:T(8,128)(2,1)}, bf16[1024,256]{1,0:T(8,128)(2,1)S(1)}, u32[]{:S(2)}, u32[]{:S(2)}) collective-permute-start(bf16[1024,256]{1,0:T(8,128)(2,1)} %get-tuple-element.104), channel_id=1, source_target_pairs={{0,1},{1,0},{2,3},{3,2},{4,5},{5,4},{6,7},{7,6},{8,9},{9,8},{10,11... | collective-permute-start | bytes 1572872 | tf_op jit(solution)/shard_map/ppermute | solution.py:595
  208.7 26.1 %collective-permute-start.25 = (bf16[1024,256]{1,0:T(8,128)(2,1)}, bf16[1024,256]{1,0:T(8,128)(2,1)S(1)}, u32[]{:S(2)}, u32[]{:S(2)}) collective-permute-start(bf16[1024,256]{1,0:T(8,128)(2,1)} %get-tuple-element.115), channel_id=1, source_target_pairs={{0,1},{1,0},{2,3},{3,2},{4,5},{5,4},{6,7},{7,6},{8,9},{9,8},{10,11... | collective-permute-start | bytes 1572872 | tf_op jit(solution)/shard_map/ppermute | solution.py:595
  210.9 32.1 %collective-permute-start.24 = (bf16[1024,256]{1,0:T(8,128)(2,1)}, bf16[1024,256]{1,0:T(8,128)(2,1)}, u32[]{:S(2)}, u32[]{:S(2)}) collective-permute-start(bf16[1024,256]{1,0:T(8,128)(2,1)} %get-tuple-element.113), channel_id=1, source_target_pairs={{0,1},{1,0},{2,3},{3,2},{4,5},{5,4},{6,7},{7,6},{8,9},{9,8},{10,11... | collective-permute-start | bytes 1572872 | tf_op jit(solution)/shard_map/ppermute | solution.py:595
  296.1 15.3 %collective-permute-start.42 = (bf16[1024,256]{1,0:T(8,128)(2,1)S(1)}, bf16[1024,256]{1,0:T(8,128)(2,1)}, u32[]{:S(2)}, u32[]{:S(2)}) collective-permute-start(bf16[1024,256]{1,0:T(8,128)(2,1)S(1)} %add_convert_fusion.8), channel_id=1, source_target_pairs={{0,2},{1,3},{2,6},{3,7},{4,0},{5,1},{6,4},{7,5},{8,10},{9,11},{10,... | collective-permute-start | bytes 1572872 | tf_op jit(solution)/shard_map/ppermute | solution.py:604
  297.7 20.9 %collective-permute-start.39 = (bf16[1024,256]{1,0:T(8,128)(2,1)}, bf16[1024,256]{1,0:T(8,128)(2,1)}, u32[]{:S(2)}, u32[]{:S(2)}) collective-permute-start(bf16[1024,256]{1,0:T(8,128)(2,1)} %get-tuple-element.143), channel_id=1, source_target_pairs={{0,1},{1,0},{2,3},{3,2},{4,5},{5,4},{6,7},{7,6},{8,9},{9,8},{10,11... | collective-permute-start | bytes 1572872 | tf_op jit(solution)/shard_map/ppermute | solution.py:595
  298.0 37.9 %collective-permute-start.38 = (bf16[1024,256]{1,0:T(8,128)(2,1)}, bf16[1024,256]{1,0:T(8,128)(2,1)}, u32[]{:S(2)}, u32[]{:S(2)}) collective-permute-start(bf16[1024,256]{1,0:T(8,128)(2,1)} %get-tuple-element.141), channel_id=1, source_target_pairs={{0,1},{1,0},{2,3},{3,2},{4,5},{5,4},{6,7},{7,6},{8,9},{9,8},{10,11... | collective-permute-start | bytes 1572872 | tf_op jit(solution)/shard_map/ppermute | solution.py:595
  316.0 91.2 %collective-permute-start.49 = (bf16[1024,256]{1,0:T(8,128)(2,1)}, bf16[1024,256]{1,0:T(8,128)(2,1)}, u32[]{:S(2)}, u32[]{:S(2)}) collective-permute-start(bf16[1024,256]{1,0:T(8,128)(2,1)} %get-tuple-element.154), channel_id=1, source_target_pairs={{8,0},{16,8},{24,16},{9,1},{17,9},{25,17},{10,2},{18,10},{26,18},{... | collective-permute-start | bytes 1572872 | tf_op jit(solution)/shard_map/ppermute | solution.py:701
  317.3 89.9 %collective-permute-start.50 = (bf16[1024,256]{1,0:T(8,128)(2,1)}, bf16[1024,256]{1,0:T(8,128)(2,1)}, u32[]{:S(2)}, u32[]{:S(2)}) collective-permute-start(bf16[1024,256]{1,0:T(8,128)(2,1)} %get-tuple-element.155), channel_id=1, source_target_pairs={{16,0},{24,8},{17,1},{25,9},{18,2},{26,10},{19,3},{27,11},{20,4},{... | collective-permute-start | bytes 1572872 | tf_op jit(solution)/shard_map/ppermute | solution.py:701
  318.6 88.6 %collective-permute-start.51 = (bf16[1024,256]{1,0:T(8,128)(2,1)}, bf16[1024,256]{1,0:T(8,128)(2,1)}, u32[]{:S(2)}, u32[]{:S(2)}) collective-permute-start(bf16[1024,256]{1,0:T(8,128)(2,1)} %get-tuple-element.156), channel_id=1, source_target_pairs={{24,0},{25,1},{26,2},{27,3},{28,4},{29,5},{30,6},{31,7}} | collective-permute-start | bytes 1572872 | tf_op jit(solution)/shard_map/ppermute | solution.py:701
  424.9 19.3 %collective-permute-start.54 = (bf16[1024,256]{1,0:T(8,128)(2,1)S(1)}, bf16[1024,256]{1,0:T(8,128)(2,1)S(1)}, u32[]{:S(2)}, u32[]{:S(2)}) collective-permute-start(bf16[1024,256]{1,0:T(8,128)(2,1)S(1)} %copy-done.32), channel_id=1, source_target_pairs={{0,1},{1,0},{2,3},{3,2},{4,5},{5,4},{6,7},{7,6},{8,9},{9,8},{10,11... | collective-permute-start | bytes 1572872 | tf_op jit(solution)/shard_map/ppermute | solution.py:595
  424.9 17.4 %collective-permute-start.60 = (f32[1024]{0:T(1024)S(1)}, f32[1024]{0:T(1024)S(1)}, u32[]{:S(2)}, u32[]{:S(2)}) collective-permute-start(f32[1024]{0:T(1024)S(1)} %add.226), channel_id=1, source_target_pairs={{0,4},{1,5},{2,0},{3,1},{4,6},{5,7},{6,2},{7,3},{8,12},{9,13},{10,... | collective-permute-start | bytes 12296 | tf_op jit(solution)/shard_map/ppermute | solution.py:604
  427.4 15.0 %collective-permute-start.59 = (f32[1024]{0:T(1024)S(1)}, f32[1024]{0:T(1024)S(1)}, u32[]{:S(2)}, u32[]{:S(2)}) collective-permute-start(f32[1024]{0:T(1024)S(1)} %add.226), channel_id=1, source_target_pairs={{0,6},{1,7},{2,4},{3,5},{4,2},{5,3},{6,0},{7,1},{8,14},{9,15},{10,... | collective-permute-start | bytes 12296 | tf_op jit(solution)/shard_map/ppermute | solution.py:604
  429.6 15.4 %collective-permute-start.56 = (bf16[1024,256]{1,0:T(8,128)(2,1)S(1)}, bf16[1024,256]{1,0:T(8,128)(2,1)S(1)}, u32[]{:S(2)}, u32[]{:S(2)}) collective-permute-start(bf16[1024,256]{1,0:T(8,128)(2,1)S(1)} %add_convert_fusion.4), channel_id=1, source_target_pairs={{0,2},{1,3},{2,6},{3,7},{4,0},{5,1},{6,4},{7,5},{8,10},{9,11},{10,... | collective-permute-start | bytes 1572872 | tf_op jit(solution)/shard_map/ppermute | solution.py:604
  442.3 23.8 %collective-permute-start.53 = (bf16[1024,256]{1,0:T(8,128)(2,1)S(1)}, bf16[1024,256]{1,0:T(8,128)(2,1)S(1)}, u32[]{:S(2)}, u32[]{:S(2)}) collective-permute-start(bf16[1024,256]{1,0:T(8,128)(2,1)S(1)} %copy-done.29), channel_id=1, source_target_pairs={{0,1},{1,0},{2,3},{3,2},{4,5},{5,4},{6,7},{7,6},{8,9},{9,8},{10,11... | collective-permute-start | bytes 1572872 | tf_op jit(solution)/shard_map/ppermute | solution.py:595
  442.4 32.4 %collective-permute-start.52 = (bf16[1024,256]{1,0:T(8,128)(2,1)S(1)}, bf16[1024,256]{1,0:T(8,128)(2,1)S(1)}, u32[]{:S(2)}, u32[]{:S(2)}) collective-permute-start(bf16[1024,256]{1,0:T(8,128)(2,1)S(1)} %copy-done.28), channel_id=1, source_target_pairs={{0,1},{1,0},{2,3},{3,2},{4,5},{5,4},{6,7},{7,6},{8,9},{9,8},{10,11... | collective-permute-start | bytes 1572872 | tf_op jit(solution)/shard_map/ppermute | solution.py:595
  445.2 20.9 %collective-permute-start.61 = (bf16[1024,256]{1,0:T(8,128)(2,1)S(1)}, bf16[1024,256]{1,0:T(8,128)(2,1)S(1)}, u32[]{:S(2)}, u32[]{:S(2)}) collective-permute-start(bf16[1024,256]{1,0:T(8,128)(2,1)S(1)} %add_convert_fusion.3), channel_id=1, source_target_pairs={{0,2},{1,3},{2,6},{3,7},{4,0},{5,1},{6,4},{7,5},{8,10},{9,11},{10,... | collective-permute-start | bytes 1572872 | tf_op jit(solution)/shard_map/ppermute | solution.py:604
  (93 other events, 1020.2 us)
Sparse Core Ops, SparseCore 0:
  50.7 48.6 all-gather.1
  243.1 164.0 all-reduce.2
